TPU v7x, 32 devices: a whole 2x2x4 slice. The times are simulated.
32 devices in a mesh: dir: 2 (over core), seq: 16 (over z, y, x).
Axes of the slice: x: 2, y: 2, z: 4, core: 2. Of those that a mesh axis runs over, the one named last changes fastest.
Arguments:
- tokens: bfloat16 [2048, 256], P('seq'), may hold values from -6 to 6
- gain: float32 [256], replicated, may hold values from 0.5 to 1.5
- w_in: bfloat16 [256, 1024], replicated, may hold values from -0.375 to 0.375
- w_out: bfloat16 [512, 256], replicated, may hold values from -0.25 to 0.25
- conv_w: float32 [2, 4, 512], P('dir'), may hold values from -3 to 3
- conv_b: float32 [2, 512], P('dir'), may hold values from -3 to 3
- w_x: bfloat16 [2, 512, 48], P('dir'), may hold values from -0.25 to 0.25
- w_dt: bfloat16 [2, 16, 512], P('dir'), may hold values from -1.5 to 1.5
- dt_bias: float32 [2, 512], P('dir'), may hold values from -9 to -1
- a_log: float32 [2, 16, 512], P('dir'), may hold values from 0 to 2.77
- d_skip: float32 [2, 512], P('dir'), may hold values from 0.5 to 1.5
- lengths: int32 [8], replicated, may hold values from 1 to 1920, as said below
- cotangent: bfloat16 [2048, 256], P('seq'), may hold values from -6 to 6
Outputs:
- out: bfloat16 [2048, 256], P('seq')
- in_grad: float32 [2048, 256], P('seq')
- grad_gain: float32 [256], replicated
- grad_w_in: float32 [256, 1024], replicated
- grad_w_out: float32 [512, 256], replicated
- grad_conv_w: float32 [2, 4, 512], P('dir')
- grad_conv_b: float32 [2, 512], P('dir')
- grad_w_x: float32 [2, 512, 48], P('dir')
- grad_w_dt: float32 [2, 16, 512], P('dir')
- grad_dt_bias: float32 [2, 512], P('dir')
- grad_a_log: float32 [2, 16, 512], P('dir')
- grad_d_skip: float32 [2, 512], P('dir')
Inputs may be any that keep to these rules, and one draw needn't show every extreme that they name: 8 window lengths that sum to 2048; the fourth has length 1920, the other 7 together hold 128 tokens, of which the first three hold at most 124, so the fourth window begins on the first index of seq and ends on the last.
All inputs are finite; a program needn't handle non-finite values.
Results may differ from a plain program's by a relative error of at most 0.011.
The roundings to bfloat16 on the way count: a program that leaves them out, or rounds other values in their place, can miss the bound.
Values may be sent and summed in bfloat16 or wider, within the bound.
A program may use at most 128 MiB of HBM per device.

v0:
```python
import functools
import math

import jax
import jax.numpy as jnp
from jax import lax
from jax.experimental import pallas as pl
from jax.experimental.pallas import tpu as pltpu
from jax.sharding import PartitionSpec as P

F32 = jnp.float32
B16 = jnp.bfloat16
MESH = pl.DeviceIdType.MESH
NORM_EPS = 1e-05
LOG2E = 1.4426950408889634
RESET = 1e6
HALO = 16
LANES = 128
GROUP = 16


def dot(a, b, ca=1, cb=0):
    return lax.dot_general(a, b, (((ca,), (cb,)), ((), ())), preferred_element_type=F32)


def silu_grad(v, sigma):
    return sigma * (1.0 + v * (1.0 - sigma))


def softplus(v):
    u = jnp.exp(-jnp.abs(v))
    s = u / (2.0 + u)
    q = s * s
    p = 1.0 / 15.0
    for k in (13.0, 11.0, 9.0, 7.0, 5.0, 3.0):
        p = p * q + 1.0 / k
    return jnp.maximum(v, 0.0) + 2.0 * s * (p * q + 1.0)


def log_split(n):
    inner = 1
    while inner * inner * 4 <= n:
        inner *= 2
    return inner, n // inner


class Ring:
    def __init__(self, ssem, rsem, size):
        self.ssem, self.rsem, self.next, self.size, self.sent = ssem, rsem, 0, size, []

    def take(self, count):
        base = self.next
        self.next += count
        assert self.next <= self.size
        return base

    def copy(self, src, dst, s, r, dev):
        return pltpu.make_async_remote_copy(
            src_ref=src, dst_ref=dst, send_sem=self.ssem.at[s], recv_sem=self.rsem.at[r],
            device_id=dev, device_id_type=MESH,
        )


class Exchange:
    def __init__(self, ring, size, me, dev):
        self.ring, self.size, self.me, self.dev = ring, size, me, dev
        self.base = ring.take(size)

    def start(self, src, dst):
        self.src, self.dst = src, dst
        for r in range(1, self.size):
            peer = lax.rem(self.me + r, self.size)
            c = self.ring.copy(src(peer), dst(self.me), self.base + r, self.base + self.me, self.dev(peer))
            c.start()
            self.ring.sent.append(c)

    def wait(self):
        for r in range(1, self.size):
            peer = lax.rem(self.me + r, self.size)
            self.ring.copy(
                self.src(peer), self.dst(peer), self.base + r, self.base + peer, self.dev(peer)
            ).wait_recv()


class Reduce:
    def __init__(self, ring, n, seq, dirn, part, total, send1, recv1, send2, recv2, buf3):
        g1, g2 = 4, 4
        g3 = n // (g1 * g2)
        self.g = (g1, g2, g3)
        lo = lax.rem(seq, g1)
        mid = lax.rem(seq // g1, g2)
        hi = seq // (g1 * g2)
        self.ids = (lo, mid, hi)
        dev1 = lambda p: (dirn, seq - lo + p)
        dev2 = lambda p: (dirn, seq + (p - mid) * g1)
        dev3 = lambda p: (dirn, seq + (p - hi) * g1 * g2)
        self.ex = [Exchange(ring, g1, lo, dev1), Exchange(ring, g2, mid, dev2)]
        self.top = Exchange(ring, g3, hi, dev3) if g3 > 1 else None
        self.back = [Exchange(ring, g2, mid, dev2), Exchange(ring, g1, lo, dev1)]
        self.part, self.total = part, total
        self.send1, self.recv1, self.send2, self.recv2, self.buf3 = send1, recv1, send2, recv2, buf3
        self.q = part.shape[0] // g1
        self.p = self.q // g2

    def scatter1(self):
        q = self.q
        self.send1[...] = self.part[...].astype(B16)
        self.ex[0].start(
            lambda p: self.send1.at[pl.ds(pl.multiple_of(p * q, q), q)], lambda s: self.recv1.at[s]
        )

    def scatter2(self):
        q, p_ = self.q, self.p
        lo, mid, _ = self.ids
        self.recv1[lo] = jnp.zeros(self.recv1.shape[1:], B16)
        self.ex[0].wait()
        acc = self.part[pl.ds(pl.multiple_of(lo * q, q), q)]
        for j in range(self.g[0]):
            acc = acc + self.recv1[j].astype(F32)
        self.part[pl.ds(0, q)] = acc
        self.send2[...] = acc.astype(B16)
        self.ex[1].start(
            lambda p: self.send2.at[pl.ds(pl.multiple_of(p * p_, p_), p_)],
            lambda s: self.recv2.at[s],
        )

    def gather2(self):
        q, p_ = self.q, self.p
        lo, mid, hi = self.ids
        self.recv2[mid] = jnp.zeros(self.recv2.shape[1:], B16)
        self.ex[1].wait()
        acc = self.part[pl.ds(pl.multiple_of(mid * p_, p_), p_)]
        for j in range(self.g[1]):
            acc = acc + self.recv2[j].astype(F32)
        if self.top is not None:
            self.buf3[hi] = acc.astype(B16)
            self.top.start(lambda p: self.buf3.at[hi], lambda s: self.buf3.at[s])
            self.top.wait()
            acc = self.buf3[0].astype(F32)
            for j in range(1, self.g[2]):
                acc = acc + self.buf3[j].astype(F32)
        at = lambda s: pl.ds(pl.multiple_of(lo * q + s * p_, p_), p_)
        self.total[at(mid)] = acc.astype(B16)
        self.back[0].start(lambda p: self.total.at[at(mid)], lambda s: self.total.at[at(s)])

    def gather1(self):
        q = self.q
        lo = self.ids[0]
        self.back[0].wait()
        at = lambda s: pl.ds(pl.multiple_of(s * q, q), q)
        self.back[1].start(lambda p: self.total.at[at(lo)], lambda s: self.total.at[at(s)])

    def finish(self):
        self.back[1].wait()


def kernel(n, nsem, *refs):
    (tok_r, gain_r, win_r, wout_r, cw_r, cb_r, wx_r, wdt_r, bias_r, alog_r, skip_r, len_r, cot_r,
     out_r, ing_r, ggain_r, gwin_r, gwout_r, gcw_r, gcb_r, gwx_r, gwdt_r, gbias_r, galog_r, gskip_r,
     thalo, brep, crep, dref, hs, lamr, rar, sdr, sar, gyr, xpad, gpad, gext, ghalo, ghsend, ghrecv,
     xin1, xsend2, xin2, yr, mgr, mbr, adjr, dtar, bsend, brecv, vsend, vrecv,
     epair, eprecv, epart, etotal, es1, er1, es2, er2, eb3,
     lpair, lprecv, lpart, ltotal, ls1, lr1, ls2, lr2, lb3, esib, lsib,
     ssem, rsem) = refs
    rows, width = tok_r.shape
    inner = wout_r.shape[0]
    state = alog_r.shape[1]
    chunks = inner // LANES
    groups = rows // GROUP
    blk = GROUP * state
    dirn = lax.axis_index("dir")
    seq = lax.axis_index("seq")
    place = seq + dirn * (n - 1 - 2 * seq)
    seq_at = lambda p: p + dirn * (n - 1 - 2 * p)
    dev_at = lambda p: (dirn, seq_at(p))
    sibling = (1 - dirn, seq)
    g_in, g_out = log_split(n)
    lo = lax.rem(place, g_in)
    hi = place // g_in
    ring = Ring(ssem, rsem, nsem)
    up = lax.rem(place + 1, n)
    down = lax.rem(place + n - 1, n)

    barrier = pltpu.get_barrier_semaphore()
    peers = [sibling, dev_at(up), dev_at(down)]
    peers += [dev_at(hi * g_in + lax.rem(lo + r, g_in)) for r in range(1, g_in)]
    peers += [dev_at(lax.rem(hi + r, g_out) * g_in + lo) for r in range(1, g_out)]
    s_lo, s_mid, s_hi = lax.rem(seq, 4), lax.rem(seq // 4, 4), seq // 16
    if n != 16:
        peers += [(dirn, seq - s_lo + lax.rem(s_lo + r, 4)) for r in range(1, 4)]
        peers += [(dirn, seq + (lax.rem(s_mid + r, 4) - s_mid) * 4) for r in range(1, 4)]
        peers += [(dirn, seq + (lax.rem(s_hi + r, n // 16) - s_hi) * 16) for r in range(1, n // 16)]
    for dev in peers:
        pl.semaphore_signal(barrier, inc=1, device_id=dev, device_id_type=MESH)
    pl.semaphore_wait(barrier, len(peers))

    edge = pl.multiple_of((1 - dirn) * (rows - HALO), HALO)
    b0 = ring.take(1)
    tok_copy = ring.copy(tok_r.at[pl.ds(edge, HALO)], thalo, b0, b0, dev_at(up))

    @pl.when(place < n - 1)
    def _():
        tok_copy.start()

    @pl.when(place == 0)
    def _():
        thalo[...] = jnp.zeros(thalo.shape, B16)

    def turn(size):
        r = lax.broadcasted_iota(jnp.int32, (size, size), 0)
        c = lax.broadcasted_iota(jnp.int32, (size, size), 1)
        return jnp.where(c == r + dirn * (size - 1 - 2 * r), 1.0, 0.0).astype(B16)

    turn_t, turn_f, turn_h = turn(rows), turn(width), turn(HALO)
    turned = lambda v, tt: dot(dot(tt, v).astype(B16), turn_f)

    def normalise(v):
        inv = lax.rsqrt(jnp.mean(v * v, axis=1, keepdims=True) + NORM_EPS)
        vr = v * inv
        return inv, vr, (vr * gain_r[...]).astype(B16)

    inv, vr, normed = normalise(turned(tok_r[...], turn_t))
    cot = turned(cot_r[...], turn_t).astype(B16)
    proj = dot(normed, win_r[...])
    xi = proj[:, :inner].astype(B16).astype(F32)
    zgate = proj[:, inner:]
    xpad[pl.ds(HALO, rows)] = xi
    sig_z = jax.nn.sigmoid(zgate)
    gate = zgate * sig_z
    gmix = dot(cot, wout_r[...], 1, 1)
    gy = gmix * gate
    gyr[...] = gy

    total = n * rows
    q = lax.broadcasted_iota(jnp.int32, (rows + 2 * HALO, LANES), 0) + (place * rows - HALO)
    dist = jnp.full(q.shape, 1 << 30, jnp.int32)
    before = jnp.int32(0)
    for w in range(len_r.shape[0]):
        after = before + len_r[w]
        delta = q - (before + dirn * (total - after - before))
        dist = jnp.where((delta >= 0) & (delta < dist), delta, dist)
        before = after
    dist = jnp.concatenate([dist] * chunks, axis=1)
    q_all = jnp.concatenate([q] * chunks, axis=1)
    dist_own = dist[HALO:HALO + rows]

    @pl.when(place > 0)
    def _():
        tok_copy.wait_recv()

    _, vr_h, normed_h = normalise(turned(thalo[...], turn_h))
    xpad[pl.ds(0, HALO)] = dot(normed_h, win_r[:, :inner]).astype(B16).astype(F32)
    conv = jnp.zeros((rows, inner), F32) + cb_r[...]
    for k in range(4):
        tap = xpad[pl.ds(HALO - k, rows)] * cw_r[0, k:k + 1]
        conv = conv + jnp.where(dist_own >= k, tap, 0.0)
    sig_c = jax.nn.sigmoid(conv)
    act_b = (conv * sig_c).astype(B16)
    act = act_b.astype(F32)
    px = dot(wx_r[0], act_b, 0, 1)
    dt_low = px[:state].astype(B16)
    b_t = px[state:2 * state]
    c_t = px[2 * state:]
    pre = dot(dt_low, wdt_r[0], 0, 0) + bias_r[...]
    step = softplus(pre)
    sd = jnp.where(dist_own == 0, RESET, step)
    sdr[...] = sd
    sar[...] = step * act
    rate = -jnp.exp(alog_r[0])
    rate2 = rate * LOG2E
    cut = lambda v: [v[:, c * LANES:(c + 1) * LANES] for c in range(chunks)]
    a2 = cut(rate2)
    a1 = cut(rate)

    def spread(g, carry):
        shift = lax.rem(LANES - g * 8, LANES)
        br = pltpu.roll(b_t, shift, 1)
        cr = pltpu.roll(c_t, shift, 1)
        for j in range(8):
            at = pl.ds(pl.multiple_of((g * 8 + j) * state, state), state)
            brep[at] = jnp.broadcast_to(br[:, j:j + 1], (state, LANES))
            crep[at] = jnp.broadcast_to(cr[:, j:j + 1], (state, LANES))
        return carry

    lax.fori_loop(0, rows // 8, spread, 0)

    def summarise(g, carry):
        h, p, l = [list(x) for x in carry]
        at8 = pl.ds(pl.multiple_of(g * 8, 8), 8)
        sd8, sa8, gy8 = sdr[at8], sar[at8], gyr[at8]
        for j in range(8):
            at = pl.ds(pl.multiple_of((g * 8 + j) * state, state), state)
            br, cr = brep[at], crep[at]
            for c in range(chunks):
                lane = slice(c * LANES, (c + 1) * LANES)
                d = jnp.exp2(sd8[j:j + 1, lane] * a2[c])
                dref[at, lane] = d
                h[c] = d * h[c] + sa8[j:j + 1, lane] * br
                p[c] = p[c] * d
                l[c] = l[c] + p[c] * (gy8[j:j + 1, lane] * cr)
        return tuple(h), tuple(p), tuple(l)

    zero = tuple(jnp.zeros((state, LANES), F32) for _ in range(chunks))
    one = tuple(jnp.ones((state, LANES), F32) for _ in range(chunks))
    h_sum, _, l_sum = lax.fori_loop(0, rows // 8, summarise, (zero, one, zero))
    join = lambda v: jnp.concatenate(v, axis=1)

    def pair_rows(v):
        top = v.astype(B16)
        rest = (v - top.astype(F32)).astype(B16)
        r = lax.broadcasted_iota(jnp.int32, (16, v.shape[1]), 0)
        both = jnp.where(r == 0, top.astype(F32), jnp.where(r == 1, rest.astype(F32), 0.0))
        return both.astype(B16)

    unpair = lambda v: v[0:1].astype(F32) + v[1:2].astype(F32)
    xin1[lo, pl.ds(0, state)] = join(h_sum).astype(B16)
    xin1[lo, pl.ds(state, state)] = join(l_sum).astype(B16)
    xin1[lo, pl.ds(2 * state, 16)] = pair_rows(jnp.sum(sd, axis=0, keepdims=True))
    ex1 = Exchange(ring, g_in, lo, lambda p: dev_at(hi * g_in + p))
    ex1.start(lambda p: xin1.at[lo], lambda s: xin1.at[s])
    ex1.wait()
    sums = [unpair(xin1[j, pl.ds(2 * state, 16)]) for j in range(g_in)]
    fwd = bwd = fwd_all = bwd_all = jnp.zeros((state, inner), F32)
    s_fwd = s_bwd = s_all = jnp.zeros((1, inner), F32)
    for j in range(g_in):
        fade = jnp.exp2(rate2 * sums[j])
        fwd_all = fade * fwd_all + xin1[j, pl.ds(0, state)].astype(F32)
        fwd = jnp.where(j < lo, fwd_all, fwd)
        s_all = s_all + sums[j]
        s_fwd = jnp.where(j < lo, s_all, s_fwd)
    for j in reversed(range(g_in)):
        fade = jnp.exp2(rate2 * sums[j])
        bwd_all = fade * bwd_all + xin1[j, pl.ds(state, state)].astype(F32)
        bwd = jnp.where(j > lo, bwd_all, bwd)
        s_bwd = jnp.where(j > lo, s_bwd + sums[j], s_bwd)
    s_pair = pair_rows(s_all)
    xsend2[0, pl.ds(0, state)] = fwd_all.astype(B16)
    xsend2[0, pl.ds(state, 16)] = s_pair
    xsend2[1, pl.ds(0, state)] = bwd_all.astype(B16)
    xsend2[1, pl.ds(state, 16)] = s_pair
    xin2[hi] = jnp.zeros(xin2.shape[1:], B16)
    ex2 = Exchange(ring, g_out, hi, lambda p: dev_at(p * g_in + lo))
    ex2.start(lambda p: xsend2.at[jnp.where(p > hi, 0, 1)], lambda s: xin2.at[s])
    ex2.wait()
    h_in = l_in = jnp.zeros((state, inner), F32)
    for k in range(g_out):
        new = jnp.exp2(rate2 * unpair(xin2[k, pl.ds(state, 16)])) * h_in
        h_in = jnp.where(k < hi, new + xin2[k, pl.ds(0, state)].astype(F32), h_in)
    for k in reversed(range(g_out)):
        new = jnp.exp2(rate2 * unpair(xin2[k, pl.ds(state, 16)])) * l_in
        l_in = jnp.where(k > hi, new + xin2[k, pl.ds(0, state)].astype(F32), l_in)
    h_in = jnp.exp2(rate2 * s_fwd) * h_in + fwd
    l_in = jnp.exp2(rate2 * s_bwd) * l_in + bwd

    hs[pl.ds(0, state)] = h_in

    def forward(g, h):
        h = list(h)
        at8 = pl.ds(pl.multiple_of(g * 8, 8), 8)
        sa8 = sar[at8]
        for j in range(8):
            at = pl.ds(pl.multiple_of((g * 8 + j) * state, state), state)
            nxt = pl.ds(pl.multiple_of((g * 8 + j + 1) * state, state), state)
            br = brep[at]
            for c in range(chunks):
                lane = slice(c * LANES, (c + 1) * LANES)
                h[c] = dref[at, lane] * h[c] + sa8[j:j + 1, lane] * br
                hs[nxt, lane] = h[c]
        return tuple(h)

    lax.fori_loop(0, rows // 8, forward, tuple(cut(h_in)))

    lane_n = lax.broadcasted_iota(jnp.int32, (state, blk), 1)
    row_n = lax.broadcasted_iota(jnp.int32, (state, blk), 0)
    rep = jnp.where(lax.rem(lane_n, state) == row_n, 1.0, 0.0).astype(B16)
    lane_t = lax.broadcasted_iota(jnp.int32, (rows, blk), 1) // state
    row_t = lax.rem(lax.broadcasted_iota(jnp.int32, (rows, blk), 0), GROUP)
    on = lane_t == row_t
    bdiag = jnp.where(on, dot(b_t.astype(B16), rep, 0, 0), 0.0).astype(B16)
    cdiag = jnp.where(on, dot(c_t.astype(B16), rep, 0, 0), 0.0).astype(B16)
    odiag = jnp.where(on, 1.0, 0.0).astype(B16)
    gy_b = gy.astype(B16)
    sa_b = (step * act).astype(B16)
    for g in range(groups):
        t = slice(g * GROUP, (g + 1) * GROUP)
        xh = hs[pl.ds(g * blk + state, blk)].astype(B16)
        yr[pl.ds(g * GROUP, GROUP)] = dot(cdiag[t], xh)
        mgr[pl.ds(g * GROUP, GROUP)] = dot(gy_b[t], xh, 1, 1)
    y = yr[...] + skip_r[...] * act
    mixed = (y * gate).astype(B16)
    bsend[...] = dot(dot(turn_t, mixed).astype(B16), dot(wout_r[...], turn_f).astype(B16))
    bb = ring.take(1)
    b_copy = ring.copy(bsend, brecv, bb, bb, sibling)
    b_copy.start()
    ring.sent.append(b_copy)
    gz = (gmix * y * silu_grad(zgate, sig_z)).astype(B16)
    gskip = jnp.sum(gy * act, axis=0, keepdims=True)

    half = width
    gwz = dot(normed, gz, 0, 0)
    gwo = dot(mixed, cot, 0, 0)
    gwo = jnp.concatenate([gwo[:width], gwo[width:]], axis=1)
    epair[0] = gwz.astype(B16)
    epair[1] = gwo.astype(B16)
    epart[...] = jnp.where(dirn == 0, gwz, gwo)
    be = ring.take(1)
    e_copy = ring.copy(epair.at[1 - dirn], eprecv, be, be, sibling)
    e_copy.start()
    ring.sent.append(e_copy)

    def backward(i, carry):
        m, acc = [list(x) for x in carry]
        g = rows // 8 - 1 - i
        at8 = pl.ds(pl.multiple_of(g * 8, 8), 8)
        sd8, gy8 = sdr[at8], gyr[at8]
        for j in reversed(range(8)):
            at = pl.ds(pl.multiple_of((g * 8 + j) * state, state), state)
            cr = crep[at]
            for c in range(chunks):
                lane = slice(c * LANES, (c + 1) * LANES)
                lam = m[c] + gy8[j:j + 1, lane] * cr
                lamr[at, lane] = lam
                m[c] = dref[at, lane] * lam
                r = m[c] * hs[at, lane] * a1[c]
                rar[at, lane] = r
                acc[c] = acc[c] + r * sd8[j:j + 1, lane]
        return tuple(m), tuple(acc)

    _, galog = lax.fori_loop(0, rows // 8, backward, (tuple(cut(l_in)), zero))
    galog = join(galog)

    early = Reduce(ring, n, seq, dirn, epart, etotal, es1, er1, es2, er2, eb3)
    e_copy.wait_recv()
    epart[...] = epart[...] + eprecv[...].astype(F32)
    early.scatter1()

    for g in range(groups):
        t = slice(g * GROUP, (g + 1) * GROUP)
        at = pl.ds(g * blk, blk)
        xl = lamr[at].astype(B16)
        adjr[pl.ds(g * GROUP, GROUP)] = dot(bdiag[t], xl)
        mbr[pl.ds(g * GROUP, GROUP)] = dot(sa_b[t], xl, 1, 1)
        dtar[pl.ds(g * GROUP, GROUP)] = dot(odiag[t], rar[at].astype(B16))
    adj = adjr[...]
    gpre = (dtar[...] + adj * act) * jax.nn.sigmoid(pre)
    gbias = jnp.sum(gpre, axis=0, keepdims=True)
    gpre = gpre.astype(B16)
    gwdt = dot(dt_low, gpre)
    pick = jnp.where(on, 1.0, 0.0)
    sel = lambda m: dot(rep, jnp.where(on, m, 0.0).astype(B16), 1, 1)
    gpx = jnp.concatenate([dot(wdt_r[0], gpre, 1, 1), sel(mbr[...]), sel(mgr[...])], axis=0).astype(B16)
    gwx_t = dot(gpx, act_b)
    gact = gy * skip_r[...] + adj * step + dot(gpx, wx_r[0], 0, 1)
    gconv_b = (gact * silu_grad(conv, sig_c)).astype(B16)
    ghsend[...] = gconv_b[:HALO]
    bh = ring.take(1)
    h_copy = ring.copy(ghsend, ghrecv, bh, bh, dev_at(down))

    @pl.when(place > 0)
    def _():
        h_copy.start()

    early.scatter2()

    gconv = gconv_b.astype(F32)
    gcb = jnp.sum(gconv, axis=0, keepdims=True)
    gcw = [
        jnp.sum(jnp.where(dist_own >= k, gconv * xpad[pl.ds(HALO - k, rows)], 0.0), axis=0, keepdims=True)
        for k in range(4)
    ]
    gpad[pl.ds(0, rows)] = gconv
    gpad[pl.ds(rows, HALO)] = jnp.zeros((HALO, inner), F32)
    gext[pl.ds(0, HALO)] = jnp.zeros((HALO, inner), F32)
    gext[pl.ds(HALO, HALO)] = gconv[:HALO]
    gxi = jnp.zeros((rows, inner), F32)
    gxe = jnp.zeros((HALO, inner), F32)
    for k in range(4):
        w = cw_r[0, k:k + 1]
        gxi = gxi + jnp.where(dist[HALO + k:HALO + k + rows] >= k, gpad[pl.ds(k, rows)] * w, 0.0)
        if k > 0:
            gxe = gxe + jnp.where(dist[k:k + HALO] >= k, gext[pl.ds(k, HALO)] * w, 0.0)
    gxi_b = jnp.concatenate([gxe, gxi], axis=0).astype(B16)
    normed_x = jnp.concatenate([normed_h, normed], axis=0)
    vr_x = jnp.concatenate([vr_h, vr], axis=0)
    gwx_half = dot(normed_x, gxi_b, 0, 0)
    gn_x = dot(gxi_b, win_r[:, :inner], 1, 1)
    gn_z = dot(gz, win_r[:, inner:], 1, 1)
    ggain = jnp.sum(gn_x * vr_x, axis=0, keepdims=True) + jnp.sum(gn_z * vr, axis=0, keepdims=True)

    own_rows = lpart.shape[0] - width // 2
    lpair[...] = gwx_half.astype(B16)
    bl = ring.take(1)
    hw = width // 2
    l_copy = ring.copy(
        lpair.at[pl.ds(pl.multiple_of((1 - dirn) * hw, hw), hw)], lprecv, bl, bl, sibling
    )
    l_copy.start()
    ring.sent.append(l_copy)
    lpart[pl.ds(0, hw)] = jnp.where(dirn == 0, gwx_half[:hw], gwx_half[hw:])
    nx = gwx_t.shape[0]
    ns = gwdt.shape[0]
    lpart[pl.ds(hw, nx)] = gwx_t
    lpart[pl.ds(hw + nx, ns)] = gwdt
    lpart[pl.ds(hw + nx + ns, state)] = galog
    pad_gain = jnp.concatenate([ggain, jnp.zeros((1, inner - width), F32)], axis=1)
    lasts = gcw + [gcb, gbias, gskip, pad_gain]
    lpart[pl.ds(hw + nx + ns + state, 8)] = jnp.concatenate(lasts, axis=0)
    spare = own_rows - nx - ns - state - 8
    lpart[pl.ds(lpart.shape[0] - spare, spare)] = jnp.zeros((spare, inner), F32)

    out_r[...] = (tok_r[...].astype(F32) + (bsend[...] + _recv(b_copy, brecv))).astype(B16)

    late = Reduce(ring, n, seq, dirn, lpart, ltotal, ls1, lr1, ls2, lr2, lb3)
    early.gather2()
    l_copy.wait_recv()
    lpart[pl.ds(0, hw)] = lpart[pl.ds(0, hw)] + lprecv[...].astype(F32)
    late.scatter1()

    @pl.when(place < n - 1)
    def _():
        h_copy.wait_recv()
        gpad[pl.ds(rows, HALO)] = ghrecv[...].astype(F32)

    edge_x = jnp.zeros((HALO, inner), F32)
    for k in range(4):
        at = HALO + rows - HALO + k
        ok = (dist[at:at + HALO] >= k) & (q_all[at:at + HALO] < total)
        edge_x = edge_x + jnp.where(ok, gpad[pl.ds(rows - HALO + k, HALO)] * cw_r[0, k:k + 1], 0.0)
    gn_edge = dot(edge_x.astype(B16), win_r[:, :inner], 1, 1)
    gn = jnp.concatenate([gn_x[HALO:rows], gn_edge], axis=0) + gn_z
    scaled = gn * gain_r[...]
    gv = inv * (scaled - vr * jnp.mean(scaled * vr, axis=1, keepdims=True))
    vsend[...] = turned(gv.astype(B16), turn_t).astype(B16)
    bv = ring.take(1)
    v_copy = ring.copy(vsend, vrecv, bv, bv, sibling)
    v_copy.start()
    ring.sent.append(v_copy)
    early.gather1()
    late.scatter2()
    early.finish()
    v_copy.wait_recv()
    ing_r[...] = cot_r[...].astype(F32) + (vsend[...].astype(F32) + vrecv[...].astype(F32))
    bs = ring.take(1)
    es_copy = ring.copy(etotal, esib, bs, bs, sibling)
    es_copy.start()
    ring.sent.append(es_copy)
    late.gather2()
    late.gather1()
    es_copy.wait_recv()

    def halves(mine, other):
        a, b = mine.astype(F32), other.astype(F32)
        return jnp.where(dirn == 0, a, b), jnp.where(dirn == 0, b, a)

    gwz_all, gwo_all = halves(etotal[...], esib[...])
    gwin_r[:, inner:] = gwz_all
    gwout_r[pl.ds(0, width)] = gwo_all[:, :width]
    gwout_r[pl.ds(width, width)] = gwo_all[:, width:]
    late.finish()
    bs2 = ring.take(1)
    ls_copy = ring.copy(ltotal, lsib, bs2, bs2, sibling)
    ls_copy.start()
    ring.sent.append(ls_copy)
    own = ltotal[pl.ds(hw, own_rows)].astype(F32)
    gwx_r[0] = own[:nx].T
    gwdt_r[0] = own[nx:nx + ns]
    galog_r[0] = own[nx + ns:nx + ns + state]
    tail = own[nx + ns + state:]
    gcw_r[0] = tail[0:4]
    gcb_r[...] = tail[4:5]
    gbias_r[...] = tail[5:6]
    gskip_r[...] = tail[6:7]
    ls_copy.wait_recv()
    low, high = halves(ltotal[pl.ds(0, hw)], lsib[pl.ds(0, hw)])
    gwin_r[pl.ds(0, hw), :inner] = low
    gwin_r[pl.ds(hw, hw), :inner] = high
    gain_at = hw + nx + ns + state
    both = ltotal[pl.ds(gain_at, 16)].astype(F32) + lsib[pl.ds(gain_at, 16)].astype(F32)
    ggain_r[...] = both[7:8, :width]

    @pl.when(place < n - 1)
    def _():
        tok_copy.wait_send()

    @pl.when(place > 0)
    def _():
        h_copy.wait_send()

    for c in ring.sent:
        c.wait_send()


def _recv(copy, ref):
    copy.wait_recv()
    return ref[...]


def on_device(n, tokens, gain, w_in, w_out, conv_w, conv_b, w_x, w_dt, dt_bias, a_log, d_skip, lengths, cotangent):
    rows, width = tokens.shape
    inner = w_out.shape[0]
    state = a_log.shape[1]
    rank = w_dt.shape[1]
    g_in, g_out = log_split(n)
    g3 = n // 16
    early_rows = width
    late_rows = -(-(width // 2 + w_x.shape[2] + rank + state + 16) // 256) * 256
    nsem = 16 + g_in + g_out + 2 * (16 + (g3 if g3 > 1 else 0))
    vm = pltpu.VMEM
    sds = jax.ShapeDtypeStruct
    half_bufs = lambda r: [
        vm((r, inner), F32), vm((r, inner), B16),
        vm((r, inner), B16), vm((4, r // 4, inner), B16),
        vm((r // 4, inner), B16), vm((4, r // 16, inner), B16),
        vm((max(g3, 1), r // 16, inner), B16),
    ]
    scratch = [
        vm((HALO, width), B16),
        vm((rows * state, LANES), F32), vm((rows * state, LANES), F32),
        vm((rows * state, inner), F32), vm(((rows + 1) * state, inner), F32),
        vm((rows * state, inner), F32), vm((rows * state, inner), F32),
        vm((rows, inner), F32), vm((rows, inner), F32), vm((rows, inner), F32),
        vm((HALO + rows, inner), F32), vm((rows + HALO, inner), F32), vm((2 * HALO, inner), F32),
        vm((HALO, inner), B16), vm((HALO, inner), B16), vm((HALO, inner), B16),
        vm((g_in, 2 * state + 16, inner), B16), vm((2, state + 16, inner), B16),
        vm((g_out, state + 16, inner), B16),
        vm((rows, inner), F32), vm((rows, GROUP * state), F32), vm((rows, GROUP * state), F32),
        vm((rows, inner), F32), vm((rows, inner), F32),
        vm((rows, width), F32), vm((rows, width), F32),
        vm((rows, width), B16), vm((rows, width), B16),
        vm((2, early_rows, inner), B16), vm((early_rows, inner), B16),
        *half_bufs(early_rows),
        vm((width, inner), B16), vm((width // 2, inner), B16),
        *half_bufs(late_rows),
        vm((early_rows, inner), B16), vm((late_rows, inner), B16),
        pltpu.SemaphoreType.DMA((nsem,)), pltpu.SemaphoreType.DMA((nsem,)),
    ]
    outs = (
        sds((rows, width), B16), sds((rows, width), F32), sds((1, width), F32),
        sds(w_in.shape, F32), sds(w_out.shape, F32), sds(conv_w.shape, F32), sds(conv_b.shape, F32),
        sds(w_x.shape, F32), sds(w_dt.shape, F32), sds(dt_bias.shape, F32), sds(a_log.shape, F32),
        sds(d_skip.shape, F32),
    )
    specs = [pl.BlockSpec(memory_space=pltpu.VMEM)] * 13
    specs[11] = pl.BlockSpec(memory_space=pltpu.SMEM)
    res = pl.pallas_call(
        functools.partial(kernel, n, nsem),
        out_shape=outs,
        in_specs=specs,
        out_specs=[pl.BlockSpec(memory_space=pltpu.VMEM)] * len(outs),
        scratch_shapes=scratch,
        compiler_params=pltpu.CompilerParams(
            collective_id=0, has_side_effects=True, vmem_limit_bytes=56 * 2**20
        ),
    )(tokens, gain.reshape(1, width), w_in, w_out, conv_w, conv_b, w_x, w_dt, dt_bias, a_log, d_skip, lengths, cotangent)
    return (res[0], res[1], res[2].reshape(width)) + tuple(res[3:])


def solution(mesh):
    d1, d2 = P("dir", None), P("dir", None, None)
    return jax.shard_map(
        functools.partial(on_device, mesh.shape["seq"]),
        mesh=mesh,
        in_specs=(P("seq", None), P(), P(), P(), d2, d1, d2, d2, d1, d2, d1, P(), P("seq", None)),
        out_specs=(P("seq", None), P("seq", None), P(), P(), P(), d2, d1, d2, d2, d1, d2, d1),
        check_vma=False,
    )
```

profile of v0, /device:TPU:1, one launch (start us, length us, event | category | flops | bytes accessed | tf_op | source)
XLA Modules:
  0.0 72.0 jit_solution(16038868845251838712)
XLA Ops:
  0.6 1.6 %copy.25.refs_6_ = bf16[1,512,48]{2,1,0:T(8,128)(2,1)} copy(bf16[1,512,48]{1,2,0:T(8,128)(2,1)} %param.19) | data formatting | bytes 98304 | tf_op args[6]
  2.2 58.9 %shard_map.220 = (bf16[128,256]{1,0:T(8,128)(2,1)}, f32[128,256]{1,0:T(8,128)}, f32[1,256]{1,0:T(1,128)}, f32[256,1024]{1,0:T(8,128)}, f32[512,256]{1,0:T(8,128)...) custom-call(bf16[128,256]{1,0:T(8,128)(2,1)} %refs_0_.1, ...), custom_call_target="tpu_custom_call" | custom-call | tf_op jit(solution)/shard_map/pallas_call | solution.py:645
  61.1 0.0 copy-start.2
  61.1 1.7 %copy.26 = f32[1,512,48]{1,2,0:T(8,128)} copy(f32[1,512,48]{2,1,0:T(8,128)} %get-tuple-element.43) | data formatting | bytes 196608
  62.9 0.0 copy-done.2
  62.9 0.6 copy.38
  63.5 0.3 copy-done.1
  63.8 0.7 copy.39
  64.4 0.0 copy-done.9
  64.4 0.6 copy.40
  65.0 2.4 %copy.41 = f32[256,1024]{1,0:T(8,128)} copy(f32[256,1024]{1,0:T(8,128)} %get-tuple-element.63) | data formatting | bytes 2097152
  67.4 0.0 copy-done
  67.4 0.8 %copy.42 = f32[512,256]{1,0:T(8,128)} copy(f32[512,256]{1,0:T(8,128)S(1)} %copy-done) | data formatting | bytes 1048576
  68.2 0.0 copy-done.5
  68.2 0.6 copy.43
  68.8 0.1 copy-done.8
  68.9 0.6 copy.44
  69.4 0.6 copy.45
  70.1 0.1 copy-done.7
  70.1 0.6 copy.46
  70.7 0.0 copy-done.3
  70.7 0.6 copy.47
  71.3 0.1 copy-done.6
  71.4 0.6 copy.48
  (10 shorter events, 0.0 us)
Async XLA Ops:
  61.1 1.7 %copy-start.2 = (bf16[128,256]{1,0:T(8,128)(2,1)S(1)}, bf16[128,256]{1,0:T(8,128)(2,1)}, u32[]{:S(2)}) copy-start(bf16[128,256]{1,0:T(8,128)(2,1)} %get-tuple-element.60) | copy-start | bytes 196612
  62.9 0.9 %copy-start.1 = (f32[128,256]{1,0:T(8,128)S(1)}, f32[128,256]{1,0:T(8,128)}, u32[]{:S(2)}) copy-start(f32[128,256]{1,0:T(8,128)} %get-tuple-element.61) | copy-start | bytes 393220
  63.8 0.7 copy-start.9
  65.0 2.4 %copy-start = (f32[512,256]{1,0:T(8,128)S(1)}, f32[512,256]{1,0:T(8,128)}, u32[]{:S(2)}) copy-start(f32[512,256]{1,0:T(8,128)} %get-tuple-element.64) | copy-start | bytes 1572868
  67.4 0.8 %copy-start.5 = (f32[1,4,512]{2,1,0:T(4,128)S(1)}, f32[1,4,512]{2,1,0:T(4,128)}, u32[]{:S(2)}) copy-start(f32[1,4,512]{2,1,0:T(4,128)} %get-tuple-element.65) | copy-start | bytes 24580
  67.4 2.1 %copy-start.4 = (f32[1,16,512]{2,1,0:T(8,128)S(1)}, f32[1,16,512]{2,1,0:T(8,128)}, u32[]{:S(2)}) copy-start(f32[1,16,512]{2,1,0:T(8,128)} %get-tuple-element.68) | copy-start | bytes 98308
  68.2 0.7 copy-start.8
  69.4 0.7 copy-start.7
  69.4 1.3 %copy-start.3 = (f32[1,16,512]{2,1,0:T(8,128)S(1)}, f32[1,16,512]{2,1,0:T(8,128)}, u32[]{:S(2)}) copy-start(f32[1,16,512]{2,1,0:T(8,128)} %get-tuple-element.70) | copy-start | bytes 98308
  70.7 0.7 copy-start.6
where the time goes:
time: 72.3 us; the launch traced here: 72 us
  Pallas kernels  58.9 us (81%)
  local copies, waits for them, and re-layouts  12.4 us (17%)
    pallas_call x1, Pallas kernels, on_device(): pl.pallas_call(functools.partial(kernel, n, nsem), out_shape=outs, in_spe...  58.9 us
    unnamed x33, local copies, waits for them, and re-layouts  12.4 us

commit v1 on v0

--- a/solution.py
+++ b/solution.py
@@ -1,5 +1,4 @@
 import functools
-import math
 
 import jax
 import jax.numpy as jnp
@@ -46,7 +45,8 @@
 
 class Ring:
     def __init__(self, ssem, rsem, size):
-        self.ssem, self.rsem, self.next, self.size, self.sent = ssem, rsem, 0, size, []
+        self.ssem, self.rsem, self.next, self.size = ssem, rsem, 0, size
+        self.sent, self.edges = [], []
 
     def take(self, count):
         base = self.next
@@ -154,13 +154,82 @@
         self.back[1].wait()
 
 
+class Direct:
+    def __init__(self, ring, n, seq, dirn, part, total, send, recv, buf3, pieces):
+        self.ring, self.part, self.total = ring, part, total
+        self.send, self.recv, self.buf3, self.pieces = send, recv, buf3, pieces
+        self.me, self.hi, self.g3 = lax.rem(seq, 16), seq // 16, n // 16
+        self.dev = lambda p: (dirn, seq - self.me + p)
+        self.s1, self.s2 = ring.take(16), ring.take(16)
+        self.top = Exchange(ring, self.g3, self.hi, lambda p: (dirn, seq + (p - self.hi) * 16)) if self.g3 > 1 else None
+        self.peers = [lax.rem(self.me + r, 16) for r in range(1, 16)]
+
+    def piece(self, p):
+        return lax.rem(p + 12, 16) if self.pieces < 16 else p
+
+    def at(self, p):
+        return pl.ds(pl.multiple_of(self.piece(p) * 16, 16), 16)
+
+    def owns(self, p, body):
+        if self.pieces < 16:
+            pl.when(self.piece(p) < self.pieces)(body)
+        else:
+            body()
+
+    def go(self, c, owner):
+        self.owns(owner, c.start)
+        if self.pieces < 16:
+            self.ring.edges.append((c, self.piece(owner) < self.pieces))
+        else:
+            self.ring.sent.append(c)
+
+    def scatter(self):
+        self.send[...] = self.part[...].astype(B16)
+        for r, p in enumerate(self.peers):
+            c = self.ring.copy(self.send.at[self.at(p)], self.recv.at[self.me], self.s1 + r, self.s1 + self.me, self.dev(p))
+            self.go(c, p)
+
+    def gather(self):
+        def add():
+            self.recv[self.me] = jnp.zeros(self.recv.shape[1:], B16)
+            for r, p in enumerate(self.peers):
+                self.ring.copy(
+                    self.send.at[pl.ds(0, 16)], self.recv.at[p], self.s1 + r, self.s1 + p, self.dev(p)
+                ).wait_recv()
+            acc = self.part[self.at(self.me)]
+            for j in range(16):
+                acc = acc + self.recv[j].astype(F32)
+            if self.top is not None:
+                self.buf3[self.hi] = acc.astype(B16)
+                self.top.start(lambda p: self.buf3.at[self.hi], lambda s: self.buf3.at[s])
+                self.top.wait()
+                for _ in range(1, self.g3):
+                    self.ring.sent.pop().wait_send()
+                acc = self.buf3[0].astype(F32)
+                for j in range(1, self.g3):
+                    acc = acc + self.buf3[j].astype(F32)
+            self.total[self.at(self.me)] = acc.astype(B16)
+
+        self.owns(self.me, add)
+        mine = self.total.at[self.at(self.me)]
+        for r, p in enumerate(self.peers):
+            self.go(self.ring.copy(mine, mine, self.s2 + r, self.s2 + self.me, self.dev(p)), self.me)
+
+    def finish(self):
+        for r, p in enumerate(self.peers):
+            there = self.total.at[self.at(p)]
+            c = self.ring.copy(there, there, self.s2 + r, self.s2 + p, self.dev(p))
+            self.owns(p, c.wait_recv)
+
+
 def kernel(n, nsem, *refs):
-    (tok_r, gain_r, win_r, wout_r, cw_r, cb_r, wx_r, wdt_r, bias_r, alog_r, skip_r, len_r, cot_r,
-     out_r, ing_r, ggain_r, gwin_r, gwout_r, gcw_r, gcb_r, gwx_r, gwdt_r, gbias_r, galog_r, gskip_r,
-     thalo, brep, crep, dref, hs, lamr, rar, sdr, sar, gyr, xpad, gpad, gext, ghalo, ghsend, ghrecv,
+    (tok_h, gain_h, win_h, wout_h, cw_h, cb_h, wx_h, wdt_h, bias_h, alog_h, skip_h, cot_h, len_r,
+     out_r, ing_r, etotal, esib, xtotal, xsib, ototal, gsib,
+     tok_r, gain_r, win_r, wout_r, cw_r, cb_r, wx_r, wdt_r, bias_r, alog_r, skip_r, cot_r, lsem,
+     thalo, brep, crep, dref, hs, lamr, rar, sdr, sar, gyr, xpad, gpad, gext, ghsend, ghrecv,
      xin1, xsend2, xin2, yr, mgr, mbr, adjr, dtar, bsend, brecv, vsend, vrecv,
-     epair, eprecv, epart, etotal, es1, er1, es2, er2, eb3,
-     lpair, lprecv, lpart, ltotal, ls1, lr1, ls2, lr2, lb3, esib, lsib,
+     epair, eprecv, epart, es1, er1, es2, er2, eb3,
+     xpair, xprecv, xpart, xs1, xr1, xb3, opart, os1, or1, ob3,
      ssem, rsem) = refs
     rows, width = tok_r.shape
     inner = wout_r.shape[0]
@@ -182,29 +251,22 @@
     down = lax.rem(place + n - 1, n)
 
     barrier = pltpu.get_barrier_semaphore()
-    peers = [sibling, dev_at(up), dev_at(down)]
-    peers += [dev_at(hi * g_in + lax.rem(lo + r, g_in)) for r in range(1, g_in)]
-    peers += [dev_at(lax.rem(hi + r, g_out) * g_in + lo) for r in range(1, g_out)]
-    s_lo, s_mid, s_hi = lax.rem(seq, 4), lax.rem(seq // 4, 4), seq // 16
+    s_lo, s_hi = lax.rem(seq, 16), seq // 16
+    peers = [sibling] + [(dirn, seq - s_lo + lax.rem(s_lo + r, 16)) for r in range(1, 16)]
     if n != 16:
-        peers += [(dirn, seq - s_lo + lax.rem(s_lo + r, 4)) for r in range(1, 4)]
-        peers += [(dirn, seq + (lax.rem(s_mid + r, 4) - s_mid) * 4) for r in range(1, 4)]
+        peers += [dev_at(up), dev_at(down)]
         peers += [(dirn, seq + (lax.rem(s_hi + r, n // 16) - s_hi) * 16) for r in range(1, n // 16)]
+        peers += [dev_at(hi * g_in + lax.rem(lo + r, g_in)) for r in range(1, g_in)]
+        peers += [dev_at(lax.rem(hi + r, g_out) * g_in + lo) for r in range(1, g_out)]
     for dev in peers:
         pl.semaphore_signal(barrier, inc=1, device_id=dev, device_id_type=MESH)
-    pl.semaphore_wait(barrier, len(peers))
-
-    edge = pl.multiple_of((1 - dirn) * (rows - HALO), HALO)
-    b0 = ring.take(1)
-    tok_copy = ring.copy(tok_r.at[pl.ds(edge, HALO)], thalo, b0, b0, dev_at(up))
-
-    @pl.when(place < n - 1)
-    def _():
-        tok_copy.start()
-
-    @pl.when(place == 0)
-    def _():
-        thalo[...] = jnp.zeros(thalo.shape, B16)
+
+    loads = {}
+    pairs = [(tok_h, tok_r), (gain_h, gain_r), (win_h, win_r), (cot_h, cot_r), (wout_h, wout_r), (cw_h, cw_r),
+             (cb_h, cb_r), (wx_h, wx_r), (wdt_h, wdt_r), (bias_h, bias_r), (alog_h, alog_r), (skip_h, skip_r)]
+    for i, (a, b) in enumerate(pairs):
+        loads[i] = pltpu.make_async_copy(a, b, lsem.at[i])
+        loads[i].start()
 
     def turn(size):
         r = lax.broadcasted_iota(jnp.int32, (size, size), 0)
@@ -213,23 +275,6 @@
 
     turn_t, turn_f, turn_h = turn(rows), turn(width), turn(HALO)
     turned = lambda v, tt: dot(dot(tt, v).astype(B16), turn_f)
-
-    def normalise(v):
-        inv = lax.rsqrt(jnp.mean(v * v, axis=1, keepdims=True) + NORM_EPS)
-        vr = v * inv
-        return inv, vr, (vr * gain_r[...]).astype(B16)
-
-    inv, vr, normed = normalise(turned(tok_r[...], turn_t))
-    cot = turned(cot_r[...], turn_t).astype(B16)
-    proj = dot(normed, win_r[...])
-    xi = proj[:, :inner].astype(B16).astype(F32)
-    zgate = proj[:, inner:]
-    xpad[pl.ds(HALO, rows)] = xi
-    sig_z = jax.nn.sigmoid(zgate)
-    gate = zgate * sig_z
-    gmix = dot(cot, wout_r[...], 1, 1)
-    gy = gmix * gate
-    gyr[...] = gy
 
     total = n * rows
     q = lax.broadcasted_iota(jnp.int32, (rows + 2 * HALO, LANES), 0) + (place * rows - HALO)
@@ -244,45 +289,75 @@
     q_all = jnp.concatenate([q] * chunks, axis=1)
     dist_own = dist[HALO:HALO + rows]
 
-    @pl.when(place > 0)
+    def normalise(v):
+        inv = lax.rsqrt(jnp.mean(v * v, axis=1, keepdims=True) + NORM_EPS)
+        vr = v * inv
+        return inv, vr, (vr * gain_r[...]).astype(B16)
+
+    for i in range(3):
+        loads[i].wait()
+    inv, vr, normed = normalise(turned(tok_r[...], turn_t))
+    proj = dot(normed, win_r[...])
+    xi = proj[:, :inner].astype(B16).astype(F32)
+    zgate = proj[:, inner:]
+    xpad[pl.ds(0, HALO)] = jnp.zeros((HALO, inner), F32)
+    xpad[pl.ds(HALO, rows)] = xi
+
+    pl.semaphore_wait(barrier, len(peers))
+    edge = pl.multiple_of((1 - dirn) * (rows - HALO), HALO)
+    b0 = ring.take(1)
+    tok_copy = ring.copy(tok_r.at[pl.ds(edge, HALO)], thalo, b0, b0, dev_at(up))
+    ring.edges.append((tok_copy, place < n - 1))
+
+    @pl.when(place < n - 1)
     def _():
-        tok_copy.wait_recv()
-
-    _, vr_h, normed_h = normalise(turned(thalo[...], turn_h))
-    xpad[pl.ds(0, HALO)] = dot(normed_h, win_r[:, :inner]).astype(B16).astype(F32)
-    conv = jnp.zeros((rows, inner), F32) + cb_r[...]
-    for k in range(4):
-        tap = xpad[pl.ds(HALO - k, rows)] * cw_r[0, k:k + 1]
-        conv = conv + jnp.where(dist_own >= k, tap, 0.0)
-    sig_c = jax.nn.sigmoid(conv)
-    act_b = (conv * sig_c).astype(B16)
-    act = act_b.astype(F32)
-    px = dot(wx_r[0], act_b, 0, 1)
-    dt_low = px[:state].astype(B16)
-    b_t = px[state:2 * state]
-    c_t = px[2 * state:]
-    pre = dot(dt_low, wdt_r[0], 0, 0) + bias_r[...]
-    step = softplus(pre)
-    sd = jnp.where(dist_own == 0, RESET, step)
-    sdr[...] = sd
-    sar[...] = step * act
+        tok_copy.start()
+
+    @pl.when(place == 0)
+    def _():
+        thalo[...] = jnp.zeros(thalo.shape, B16)
+
+    for i in range(3, len(pairs)):
+        loads[i].wait()
+    cot = turned(cot_r[...], turn_t).astype(B16)
+    sig_z = jax.nn.sigmoid(zgate)
+    gate = zgate * sig_z
+    gmix = dot(cot, wout_r[...], 1, 1)
+    gy = gmix * gate
+    gyr[...] = gy
     rate = -jnp.exp(alog_r[0])
     rate2 = rate * LOG2E
     cut = lambda v: [v[:, c * LANES:(c + 1) * LANES] for c in range(chunks)]
     a2 = cut(rate2)
     a1 = cut(rate)
 
-    def spread(g, carry):
-        shift = lax.rem(LANES - g * 8, LANES)
-        br = pltpu.roll(b_t, shift, 1)
-        cr = pltpu.roll(c_t, shift, 1)
-        for j in range(8):
-            at = pl.ds(pl.multiple_of((g * 8 + j) * state, state), state)
-            brep[at] = jnp.broadcast_to(br[:, j:j + 1], (state, LANES))
-            crep[at] = jnp.broadcast_to(cr[:, j:j + 1], (state, LANES))
-        return carry
-
-    lax.fori_loop(0, rows // 8, spread, 0)
+    def drive(count):
+        conv = jnp.zeros((count, inner), F32) + cb_r[...]
+        for k in range(4):
+            tap = xpad[pl.ds(HALO - k, count)] * cw_r[0, k:k + 1]
+            conv = conv + jnp.where(dist_own[:count] >= k, tap, 0.0)
+        sig_c = jax.nn.sigmoid(conv)
+        act_b = (conv * sig_c).astype(B16)
+        px = dot(wx_r[0], act_b, 1, 1)
+        pre = dot(px[:state].astype(B16), wdt_r[0], 0, 0) + bias_r[...]
+        step = softplus(pre)
+        sd = jnp.where(dist_own[:count] == 0, RESET, step)
+        sdr[pl.ds(0, count)] = sd
+        sar[pl.ds(0, count)] = step * act_b.astype(F32)
+        return conv, sig_c, act_b, px, pre, step, sd
+
+    def spread(b_t, c_t, first, last):
+        def body(g, carry):
+            shift = lax.rem(LANES - g * 8, LANES)
+            br = pltpu.roll(b_t, shift, 1)
+            cr = pltpu.roll(c_t, shift, 1)
+            for j in range(8):
+                at = pl.ds(pl.multiple_of((g * 8 + j) * state, state), state)
+                brep[at] = jnp.broadcast_to(br[:, j:j + 1], (state, LANES))
+                crep[at] = jnp.broadcast_to(cr[:, j:j + 1], (state, LANES))
+            return carry
+
+        lax.fori_loop(first, last, body, 0)
 
     def summarise(g, carry):
         h, p, l = [list(x) for x in carry]
@@ -302,8 +377,33 @@
 
     zero = tuple(jnp.zeros((state, LANES), F32) for _ in range(chunks))
     one = tuple(jnp.ones((state, LANES), F32) for _ in range(chunks))
-    h_sum, _, l_sum = lax.fori_loop(0, rows // 8, summarise, (zero, one, zero))
     join = lambda v: jnp.concatenate(v, axis=1)
+    head = HALO // 8
+
+    whole = drive(rows)
+    spread(whole[3][state:2 * state], whole[3][2 * state:], head, rows // 8)
+    h_late, p_late, l_late = lax.fori_loop(head, rows // 8, summarise, (zero, one, zero))
+
+    @pl.when(place > 0)
+    def _():
+        tok_copy.wait_recv()
+
+    _, vr_h, normed_h = normalise(turned(thalo[...], turn_h))
+    xpad[pl.ds(0, HALO)] = dot(normed_h, win_r[:, :inner]).astype(B16).astype(F32)
+    start = drive(HALO)
+    first_px = jnp.concatenate([start[3], jnp.zeros((start[3].shape[0], rows - HALO), F32)], axis=1)
+    lane_px = lax.broadcasted_iota(jnp.int32, first_px.shape, 1)
+    px = jnp.where(lane_px < HALO, first_px, whole[3])
+    patch = lambda i: jnp.concatenate([start[i], whole[i][HALO:]], axis=0)
+    conv, sig_c, act_b, pre, step, sd = [patch(i) for i in (0, 1, 2, 4, 5, 6)]
+    act = act_b.astype(F32)
+    dt_low = px[:state].astype(B16)
+    b_t = px[state:2 * state]
+    c_t = px[2 * state:]
+    spread(b_t, c_t, 0, head)
+    h_first, p_first, l_first = lax.fori_loop(0, head, summarise, (zero, one, zero))
+    h_sum = join(h_late) + join(p_late) * join(h_first)
+    l_sum = join(l_first) + join(p_first) * join(l_late)
 
     def pair_rows(v):
         top = v.astype(B16)
@@ -313,8 +413,8 @@
         return both.astype(B16)
 
     unpair = lambda v: v[0:1].astype(F32) + v[1:2].astype(F32)
-    xin1[lo, pl.ds(0, state)] = join(h_sum).astype(B16)
-    xin1[lo, pl.ds(state, state)] = join(l_sum).astype(B16)
+    xin1[lo, pl.ds(0, state)] = h_sum.astype(B16)
+    xin1[lo, pl.ds(state, state)] = l_sum.astype(B16)
     xin1[lo, pl.ds(2 * state, 16)] = pair_rows(jnp.sum(sd, axis=0, keepdims=True))
     ex1 = Exchange(ring, g_in, lo, lambda p: dev_at(hi * g_in + p))
     ex1.start(lambda p: xin1.at[lo], lambda s: xin1.at[s])
@@ -388,15 +488,9 @@
         mgr[pl.ds(g * GROUP, GROUP)] = dot(gy_b[t], xh, 1, 1)
     y = yr[...] + skip_r[...] * act
     mixed = (y * gate).astype(B16)
-    bsend[...] = dot(dot(turn_t, mixed).astype(B16), dot(wout_r[...], turn_f).astype(B16))
-    bb = ring.take(1)
-    b_copy = ring.copy(bsend, brecv, bb, bb, sibling)
-    b_copy.start()
-    ring.sent.append(b_copy)
     gz = (gmix * y * silu_grad(zgate, sig_z)).astype(B16)
     gskip = jnp.sum(gy * act, axis=0, keepdims=True)
 
-    half = width
     gwz = dot(normed, gz, 0, 0)
     gwo = dot(mixed, cot, 0, 0)
     gwo = jnp.concatenate([gwo[:width], gwo[width:]], axis=1)
@@ -407,6 +501,11 @@
     e_copy = ring.copy(epair.at[1 - dirn], eprecv, be, be, sibling)
     e_copy.start()
     ring.sent.append(e_copy)
+    bsend[...] = dot(dot(turn_t, mixed).astype(B16), dot(wout_r[...], turn_f).astype(B16))
+    bb = ring.take(1)
+    b_copy = ring.copy(bsend, brecv, bb, bb, sibling)
+    b_copy.start()
+    ring.sent.append(b_copy)
 
     def backward(i, carry):
         m, acc = [list(x) for x in carry]
@@ -446,28 +545,13 @@
     gbias = jnp.sum(gpre, axis=0, keepdims=True)
     gpre = gpre.astype(B16)
     gwdt = dot(dt_low, gpre)
-    pick = jnp.where(on, 1.0, 0.0)
     sel = lambda m: dot(rep, jnp.where(on, m, 0.0).astype(B16), 1, 1)
     gpx = jnp.concatenate([dot(wdt_r[0], gpre, 1, 1), sel(mbr[...]), sel(mgr[...])], axis=0).astype(B16)
     gwx_t = dot(gpx, act_b)
-    gact = gy * skip_r[...] + adj * step + dot(gpx, wx_r[0], 0, 1)
+    gact = gy * skip_r[...] + adj * step + dot(gpx, wx_r[0], 0, 0)
     gconv_b = (gact * silu_grad(conv, sig_c)).astype(B16)
-    ghsend[...] = gconv_b[:HALO]
-    bh = ring.take(1)
-    h_copy = ring.copy(ghsend, ghrecv, bh, bh, dev_at(down))
-
-    @pl.when(place > 0)
-    def _():
-        h_copy.start()
-
-    early.scatter2()
-
     gconv = gconv_b.astype(F32)
-    gcb = jnp.sum(gconv, axis=0, keepdims=True)
-    gcw = [
-        jnp.sum(jnp.where(dist_own >= k, gconv * xpad[pl.ds(HALO - k, rows)], 0.0), axis=0, keepdims=True)
-        for k in range(4)
-    ]
+
     gpad[pl.ds(0, rows)] = gconv
     gpad[pl.ds(rows, HALO)] = jnp.zeros((HALO, inner), F32)
     gext[pl.ds(0, HALO)] = jnp.zeros((HALO, inner), F32)
@@ -483,38 +567,50 @@
     normed_x = jnp.concatenate([normed_h, normed], axis=0)
     vr_x = jnp.concatenate([vr_h, vr], axis=0)
     gwx_half = dot(normed_x, gxi_b, 0, 0)
+    hw = inner // 2
+    left, right = gwx_half[:, :hw], gwx_half[:, hw:]
+    xpair[0] = left.astype(B16)
+    xpair[1] = right.astype(B16)
+    bx = ring.take(1)
+    x_copy = ring.copy(xpair.at[1 - dirn], xprecv, bx, bx, sibling)
+    x_copy.start()
+    ring.sent.append(x_copy)
+    xpart[...] = jnp.where(dirn == 0, left, right)
+    ghsend[...] = gconv_b[:HALO]
+    bh = ring.take(1)
+    h_copy = ring.copy(ghsend, ghrecv, bh, bh, dev_at(down))
+    ring.edges.append((h_copy, place > 0))
+
+    @pl.when(place > 0)
+    def _():
+        h_copy.start()
+
     gn_x = dot(gxi_b, win_r[:, :inner], 1, 1)
     gn_z = dot(gz, win_r[:, inner:], 1, 1)
     ggain = jnp.sum(gn_x * vr_x, axis=0, keepdims=True) + jnp.sum(gn_z * vr, axis=0, keepdims=True)
-
-    own_rows = lpart.shape[0] - width // 2
-    lpair[...] = gwx_half.astype(B16)
-    bl = ring.take(1)
-    hw = width // 2
-    l_copy = ring.copy(
-        lpair.at[pl.ds(pl.multiple_of((1 - dirn) * hw, hw), hw)], lprecv, bl, bl, sibling
-    )
-    l_copy.start()
-    ring.sent.append(l_copy)
-    lpart[pl.ds(0, hw)] = jnp.where(dirn == 0, gwx_half[:hw], gwx_half[hw:])
-    nx = gwx_t.shape[0]
-    ns = gwdt.shape[0]
-    lpart[pl.ds(hw, nx)] = gwx_t
-    lpart[pl.ds(hw + nx, ns)] = gwdt
-    lpart[pl.ds(hw + nx + ns, state)] = galog
+    gcb = jnp.sum(gconv, axis=0, keepdims=True)
+    gcw = [
+        jnp.sum(jnp.where(dist_own >= k, gconv * xpad[pl.ds(HALO - k, rows)], 0.0), axis=0, keepdims=True)
+        for k in range(4)
+    ]
     pad_gain = jnp.concatenate([ggain, jnp.zeros((1, inner - width), F32)], axis=1)
-    lasts = gcw + [gcb, gbias, gskip, pad_gain]
-    lpart[pl.ds(hw + nx + ns + state, 8)] = jnp.concatenate(lasts, axis=0)
-    spare = own_rows - nx - ns - state - 8
-    lpart[pl.ds(lpart.shape[0] - spare, spare)] = jnp.zeros((spare, inner), F32)
-
-    out_r[...] = (tok_r[...].astype(F32) + (bsend[...] + _recv(b_copy, brecv))).astype(B16)
-
-    late = Reduce(ring, n, seq, dirn, lpart, ltotal, ls1, lr1, ls2, lr2, lb3)
-    early.gather2()
-    l_copy.wait_recv()
-    lpart[pl.ds(0, hw)] = lpart[pl.ds(0, hw)] + lprecv[...].astype(F32)
-    late.scatter1()
+    tail = jnp.concatenate(gcw + [gcb, gbias, gskip, pad_gain], axis=0)
+    row = 0
+    for part in (gwx_t, gwdt, galog, tail):
+        k = part.shape[0]
+        opart[pl.ds(row, k)] = part[:, :hw]
+        opart[pl.ds(row + k, k)] = part[:, hw:]
+        row += 2 * k
+    opart[pl.ds(row, opart.shape[0] - row)] = jnp.zeros((opart.shape[0] - row, hw), F32)
+    own = Direct(ring, n, seq, dirn, opart, ototal, os1, or1, ob3, -(-row // 16))
+    own.scatter()
+    xlate = Direct(ring, n, seq, dirn, xpart, xtotal, xs1, xr1, xb3, 16)
+    x_copy.wait_recv()
+    xpart[...] = xpart[...] + xprecv[...].astype(F32)
+    xlate.scatter()
+    early.scatter2()
+    b_copy.wait_recv()
+    out_r[...] = (tok_r[...].astype(F32) + (bsend[...] + brecv[...])).astype(B16)
 
     @pl.when(place < n - 1)
     def _():
@@ -535,64 +631,91 @@
     v_copy = ring.copy(vsend, vrecv, bv, bv, sibling)
     v_copy.start()
     ring.sent.append(v_copy)
+    early.gather2()
+    own.gather()
+    xlate.gather()
     early.gather1()
-    late.scatter2()
-    early.finish()
     v_copy.wait_recv()
     ing_r[...] = cot_r[...].astype(F32) + (vsend[...].astype(F32) + vrecv[...].astype(F32))
+    early.finish()
     bs = ring.take(1)
     es_copy = ring.copy(etotal, esib, bs, bs, sibling)
     es_copy.start()
     ring.sent.append(es_copy)
-    late.gather2()
-    late.gather1()
+    own.finish()
+    bo = ring.take(1)
+    gat = pl.ds(row - 16, 16)
+    os_copy = ring.copy(ototal.at[gat], gsib, bo, bo, sibling)
+    os_copy.start()
+    ring.sent.append(os_copy)
+    xlate.finish()
+    bs2 = ring.take(1)
+    xs_copy = ring.copy(xtotal, xsib, bs2, bs2, sibling)
+    xs_copy.start()
+    ring.sent.append(xs_copy)
     es_copy.wait_recv()
-
-    def halves(mine, other):
-        a, b = mine.astype(F32), other.astype(F32)
-        return jnp.where(dirn == 0, a, b), jnp.where(dirn == 0, b, a)
-
-    gwz_all, gwo_all = halves(etotal[...], esib[...])
-    gwin_r[:, inner:] = gwz_all
-    gwout_r[pl.ds(0, width)] = gwo_all[:, :width]
-    gwout_r[pl.ds(width, width)] = gwo_all[:, width:]
-    late.finish()
-    bs2 = ring.take(1)
-    ls_copy = ring.copy(ltotal, lsib, bs2, bs2, sibling)
-    ls_copy.start()
-    ring.sent.append(ls_copy)
-    own = ltotal[pl.ds(hw, own_rows)].astype(F32)
-    gwx_r[0] = own[:nx].T
-    gwdt_r[0] = own[nx:nx + ns]
-    galog_r[0] = own[nx + ns:nx + ns + state]
-    tail = own[nx + ns + state:]
-    gcw_r[0] = tail[0:4]
-    gcb_r[...] = tail[4:5]
-    gbias_r[...] = tail[5:6]
-    gskip_r[...] = tail[6:7]
-    ls_copy.wait_recv()
-    low, high = halves(ltotal[pl.ds(0, hw)], lsib[pl.ds(0, hw)])
-    gwin_r[pl.ds(0, hw), :inner] = low
-    gwin_r[pl.ds(hw, hw), :inner] = high
-    gain_at = hw + nx + ns + state
-    both = ltotal[pl.ds(gain_at, 16)].astype(F32) + lsib[pl.ds(gain_at, 16)].astype(F32)
-    ggain_r[...] = both[7:8, :width]
-
-    @pl.when(place < n - 1)
-    def _():
-        tok_copy.wait_send()
-
-    @pl.when(place > 0)
-    def _():
-        h_copy.wait_send()
-
+    os_copy.wait_recv()
+    xs_copy.wait_recv()
+    done_edges(ring)
     for c in ring.sent:
         c.wait_send()
 
 
-def _recv(copy, ref):
-    copy.wait_recv()
-    return ref[...]
+def finish(sizes, *refs):
+    (out_v, ing_v, etotal, esib, xtotal, xsib, ototal, gsib,
+     out_h, ing_h, ggain_h, gwin_h, gwout_h, gcw_h, gcb_h, gwx_h, gwdt_h, gbias_h, galog_h, gskip_h,
+     ggain, gwin, gwout, gcw, gcb, gwx, gwdt, gbias, galog, gskip, sems) = refs
+    nx, ns, state = sizes
+    dirn = lax.axis_index("dir")
+    width = ing_v.shape[1]
+    hw = xtotal.shape[1]
+    inner = 2 * hw
+    started = []
+
+    def write(src, dst):
+        c = pltpu.make_async_copy(src, dst, sems.at[len(started)])
+        c.start()
+        started.append(c)
+
+    write(out_v, out_h)
+    write(ing_v, ing_h)
+
+    def halves(mine, other):
+        a, b = mine[...].astype(F32), other[...].astype(F32)
+        return jnp.where(dirn == 0, a, b), jnp.where(dirn == 0, b, a)
+
+    gz, go = halves(etotal, esib)
+    gwout[pl.ds(0, width)] = go[:, :width]
+    gwout[pl.ds(width, width)] = go[:, width:]
+    write(gwout, gwout_h)
+    gwin[:, inner:] = gz
+    left, right = halves(xtotal, xsib)
+    gwin[:, :hw] = left
+    gwin[:, hw:inner] = right
+    write(gwin, gwin_h)
+    row = 0
+    parts = []
+    for k in (nx, ns, state, 8):
+        parts.append(jnp.concatenate([ototal[pl.ds(row, k)], ototal[pl.ds(row + k, k)]], axis=1).astype(F32))
+        row += 2 * k
+    tail = parts[3]
+    gwx[0], gwdt[0], galog[0] = parts[:3]
+    gcw[0] = tail[0:4]
+    gcb[...], gbias[...], gskip[...] = tail[4:5], tail[5:6], tail[6:7]
+    both = ototal[pl.ds(row - 16, 16)].astype(F32) + gsib[...].astype(F32)
+    ggain[...] = both[7:8, :width]
+    for a, b in ((gwx, gwx_h), (gwdt, gwdt_h), (galog, galog_h), (gcw, gcw_h), (gcb, gcb_h),
+                 (gbias, gbias_h), (gskip, gskip_h), (ggain, ggain_h)):
+        write(a, b)
+    for c in started:
+        c.wait()
+
+
+def done_edges(ring):
+    for c, cond in ring.edges:
+        @pl.when(cond)
+        def _():
+            c.wait_send()
 
 
 def on_device(n, tokens, gain, w_in, w_out, conv_w, conv_b, w_x, w_dt, dt_bias, a_log, d_skip, lengths, cotangent):
@@ -601,58 +724,67 @@
     state = a_log.shape[1]
     rank = w_dt.shape[1]
     g_in, g_out = log_split(n)
-    g3 = n // 16
-    early_rows = width
-    late_rows = -(-(width // 2 + w_x.shape[2] + rank + state + 16) // 256) * 256
-    nsem = 16 + g_in + g_out + 2 * (16 + (g3 if g3 > 1 else 0))
+    g3 = max(n // 16, 1)
+    hw = inner // 2
+    gain = gain.reshape(1, width)
+    w_xt = jnp.swapaxes(w_x, 1, 2)
+    nsem = 16 + g_in + g_out + 16 + 4 * 16 + 3 * g3
     vm = pltpu.VMEM
     sds = jax.ShapeDtypeStruct
-    half_bufs = lambda r: [
-        vm((r, inner), F32), vm((r, inner), B16),
-        vm((r, inner), B16), vm((4, r // 4, inner), B16),
-        vm((r // 4, inner), B16), vm((4, r // 16, inner), B16),
-        vm((max(g3, 1), r // 16, inner), B16),
-    ]
-    scratch = [
+    ins = (tokens, gain, w_in, w_out, conv_w, conv_b, w_xt, w_dt, dt_bias, a_log, d_skip, cotangent)
+    direct = [vm((256, hw), F32), vm((256, hw), B16), vm((16, 16, hw), B16), vm((g3, 16, hw), B16)]
+    scratch = [vm(x.shape, x.dtype) for x in ins] + [
+        pltpu.SemaphoreType.DMA((len(ins),)),
         vm((HALO, width), B16),
         vm((rows * state, LANES), F32), vm((rows * state, LANES), F32),
         vm((rows * state, inner), F32), vm(((rows + 1) * state, inner), F32),
         vm((rows * state, inner), F32), vm((rows * state, inner), F32),
         vm((rows, inner), F32), vm((rows, inner), F32), vm((rows, inner), F32),
         vm((HALO + rows, inner), F32), vm((rows + HALO, inner), F32), vm((2 * HALO, inner), F32),
-        vm((HALO, inner), B16), vm((HALO, inner), B16), vm((HALO, inner), B16),
+        vm((HALO, inner), B16), vm((HALO, inner), B16),
         vm((g_in, 2 * state + 16, inner), B16), vm((2, state + 16, inner), B16),
         vm((g_out, state + 16, inner), B16),
         vm((rows, inner), F32), vm((rows, GROUP * state), F32), vm((rows, GROUP * state), F32),
         vm((rows, inner), F32), vm((rows, inner), F32),
         vm((rows, width), F32), vm((rows, width), F32),
         vm((rows, width), B16), vm((rows, width), B16),
-        vm((2, early_rows, inner), B16), vm((early_rows, inner), B16),
-        *half_bufs(early_rows),
-        vm((width, inner), B16), vm((width // 2, inner), B16),
-        *half_bufs(late_rows),
-        vm((early_rows, inner), B16), vm((late_rows, inner), B16),
+        vm((2, width, inner), B16), vm((width, inner), B16), vm((width, inner), F32),
+        vm((width, inner), B16), vm((4, width // 4, inner), B16),
+        vm((width // 4, inner), B16), vm((4, width // 16, inner), B16), vm((g3, width // 16, inner), B16),
+        vm((2, width, hw), B16), vm((width, hw), B16), *direct, *direct,
         pltpu.SemaphoreType.DMA((nsem,)), pltpu.SemaphoreType.DMA((nsem,)),
     ]
+    mids = [
+        vm((rows, width), B16), vm((rows, width), F32), vm((width, inner), B16), vm((width, inner), B16),
+        vm((width, hw), B16), vm((width, hw), B16), vm((256, hw), B16), vm((16, hw), B16),
+    ]
+    in_vmem = pl.BlockSpec(memory_space=pltpu.VMEM)
+    in_hbm = pl.BlockSpec(memory_space=pltpu.HBM)
+    sums = pl.pallas_call(
+        functools.partial(kernel, n, nsem),
+        out_shape=mids,
+        in_specs=[in_hbm] * len(ins) + [pl.BlockSpec(memory_space=pltpu.SMEM)],
+        out_specs=[in_vmem] * len(mids),
+        scratch_shapes=scratch,
+        compiler_params=pltpu.CompilerParams(
+            collective_id=0, has_side_effects=True, vmem_limit_bytes=40 * 2**20
+        ),
+    )(*ins, lengths)
     outs = (
         sds((rows, width), B16), sds((rows, width), F32), sds((1, width), F32),
         sds(w_in.shape, F32), sds(w_out.shape, F32), sds(conv_w.shape, F32), sds(conv_b.shape, F32),
-        sds(w_x.shape, F32), sds(w_dt.shape, F32), sds(dt_bias.shape, F32), sds(a_log.shape, F32),
+        sds(w_xt.shape, F32), sds(w_dt.shape, F32), sds(dt_bias.shape, F32), sds(a_log.shape, F32),
         sds(d_skip.shape, F32),
     )
-    specs = [pl.BlockSpec(memory_space=pltpu.VMEM)] * 13
-    specs[11] = pl.BlockSpec(memory_space=pltpu.SMEM)
     res = pl.pallas_call(
-        functools.partial(kernel, n, nsem),
+        functools.partial(finish, (w_xt.shape[1], rank, state)),
         out_shape=outs,
-        in_specs=specs,
-        out_specs=[pl.BlockSpec(memory_space=pltpu.VMEM)] * len(outs),
-        scratch_shapes=scratch,
-        compiler_params=pltpu.CompilerParams(
-            collective_id=0, has_side_effects=True, vmem_limit_bytes=56 * 2**20
-        ),
-    )(tokens, gain.reshape(1, width), w_in, w_out, conv_w, conv_b, w_x, w_dt, dt_bias, a_log, d_skip, lengths, cotangent)
-    return (res[0], res[1], res[2].reshape(width)) + tuple(res[3:])
+        in_specs=[in_vmem] * len(mids),
+        out_specs=[in_hbm] * len(outs),
+        scratch_shapes=[vm(x.shape, x.dtype) for x in outs[2:]] + [pltpu.SemaphoreType.DMA((len(outs),))],
+        compiler_params=pltpu.CompilerParams(vmem_limit_bytes=8 * 2**20),
+    )(*sums)
+    return (res[0], res[1], res[2].reshape(width)) + tuple(res[3:7]) + (jnp.swapaxes(res[7], 1, 2),) + tuple(res[8:])
 
 
 def solution(mesh):

time: 72.3 us -> 59.8 us (0.83)
  Pallas kernels: 58.9 us -> 49.8 us
  local copies, waits for them, and re-layouts: 12.4 us -> 8.67 us
    pallas_call x1 -> x2, Pallas kernels: 58.9 us -> 49.8 us  [the longest x1 48.5 us: on_device(): pl.pallas_call(functools.partial(kernel, n, nsem), out_shape=mids, in_spe...]
    unnamed x33 -> x26, local copies, waits for them, and re-layouts: 12.4 us -> 8.67 us
where the time goes in v1:
time: 59.8 us; the launch traced here: 59.2 us
  Pallas kernels  49.8 us (83%)
  local copies, waits for them, and re-layouts  8.67 us (14%)
  between operations  0.69 us (1%)
    pallas_call x1, Pallas kernels, on_device(): pl.pallas_call(functools.partial(kernel, n, nsem), out_shape=mids, in_spe...  48.5 us
    unnamed x26, local copies, waits for them, and re-layouts  8.67 us
    pallas_call x1, Pallas kernels, on_device(): pl.pallas_call(functools.partial(finish, (w_xt.shape[1], rank, state)), o...  1.38 us

profile of v1, /device:TPU:1, one launch (start us, length us, event | category | flops | bytes accessed | tf_op | source)
XLA Modules:
  0.0 59.2 jit_solution(14904630279413419236)
XLA Ops:
  0.6 0.0 copy-start.8
  0.7 0.0 copy-start.11
  0.7 0.0 copy-start.12
  0.7 0.7 %copy-done.8 = f32[1,512]{1,0:T(1,128)S(1)} copy-done((f32[1,512]{1,0:T(1,128)S(1)}, f32[1,512]{1,0:T(1,128)}, u32[]{:S(2)}) %copy-start.8) | copy-done | bytes 2072
  1.3 0.0 copy-done.11
  1.3 0.0 copy-done.12
  1.3 0.0 copy-start
  1.4 1.0 %copy-done = bf16[256,1024]{1,0:T(8,128)(2,1)S(1)} copy-done((bf16[256,1024]{1,0:T(8,128)(2,1)S(1)}, bf16[256,1024]{1,0:T(8,128)(2,1)}, u32[]{:S(2)}) %copy-start) | copy-done | bytes 524312
  2.4 0.0 copy-start.1
  2.4 0.9 %copy-done.1 = bf16[512,256]{1,0:T(8,128)(2,1)S(1)} copy-done((bf16[512,256]{1,0:T(8,128)(2,1)S(1)}, bf16[512,256]{1,0:T(8,128)(2,1)}, u32[]{:S(2)}) %copy-start.1) | copy-done | bytes 262168
  3.3 0.8 %copy-done.2 = bf16[128,256]{1,0:T(8,128)(2,1)S(1)} copy-done((bf16[128,256]{1,0:T(8,128)(2,1)S(1)}, bf16[128,256]{1,0:T(8,128)(2,1)}, u32[]{:S(2)}) %copy-start.2) | copy-done | bytes 65560
  4.2 0.8 %copy-done.3 = bf16[128,256]{1,0:T(8,128)(2,1)S(1)} copy-done((bf16[128,256]{1,0:T(8,128)(2,1)S(1)}, bf16[128,256]{1,0:T(8,128)(2,1)}, u32[]{:S(2)}) %copy-start.3) | copy-done | bytes 65560
  5.0 0.8 %copy-done.4 = bf16[1,512,48]{1,2,0:T(8,128)(2,1)S(1)} copy-done((bf16[1,512,48]{1,2,0:T(8,128)(2,1)S(1)}, bf16[1,512,48]{1,2,0:T(8,128)(2,1)}, u32[]{:S(2)}) %copy-start.4) | copy-done | bytes 49176
  5.8 0.0 copy-start.5
  5.8 0.8 %copy-done.5 = f32[1,16,512]{2,1,0:T(8,128)S(1)} copy-done((f32[1,16,512]{2,1,0:T(8,128)S(1)}, f32[1,16,512]{2,1,0:T(8,128)}, u32[]{:S(2)}) %copy-start.5) | copy-done | bytes 32792
  6.6 0.0 copy-start.6
  6.6 0.7 %copy-done.6 = bf16[1,16,512]{2,1,0:T(8,128)(2,1)S(1)} copy-done((bf16[1,16,512]{2,1,0:T(8,128)(2,1)S(1)}, bf16[1,16,512]{2,1,0:T(8,128)(2,1)}, u32[]{:S(2)}) %copy-start.6) | copy-done | bytes 16408
  7.3 0.0 copy-start.7
  7.3 0.7 %copy-done.7 = f32[1,4,512]{2,1,0:T(4,128)S(1)} copy-done((f32[1,4,512]{2,1,0:T(4,128)S(1)}, f32[1,4,512]{2,1,0:T(4,128)}, u32[]{:S(2)}) %copy-start.7) | copy-done | bytes 8216
  8.0 0.0 copy-start.9
  8.0 0.7 %copy-done.9 = f32[1,512]{1,0:T(1,128)S(1)} copy-done((f32[1,512]{1,0:T(1,128)S(1)}, f32[1,512]{1,0:T(1,128)}, u32[]{:S(2)}) %copy-start.9) | copy-done | bytes 2072
  8.7 0.7 %copy-done.10 = f32[1,512]{1,0:T(1,128)S(1)} copy-done((f32[1,512]{1,0:T(1,128)S(1)}, f32[1,512]{1,0:T(1,128)}, u32[]{:S(2)}) %copy-start.10) | copy-done | bytes 2072
  9.4 48.5 %shard_map.220 = (bf16[128,256]{1,0:T(8,128)(2,1)S(1)}, f32[128,256]{1,0:T(8,128)S(1)}, bf16[256,512]{1,0:T(8,128)(2,1)S(1)}, bf16[256,512]{1,0:T(8,128)(2,1)S(1...) custom-call(bf16[128,256]{1,0:T(8,128)(2,1)S(1)} %copy-done.2, ...), custom_call_target="tpu_custom_call" | custom-call | tf_op jit(solution)/shard_map/pallas_call | solution.py:763
  57.8 1.4 %shard_map.221 = (bf16[128,256]{1,0:T(8,128)(2,1)}, f32[128,256]{1,0:T(8,128)}, f32[1,256]{1,0:T(1,128)}, f32[256,1024]{1,0:T(8,128)}, f32[512,256]{1,0:T(8,128)...) custom-call(bf16[128,256]{1,0:T(8,128)(2,1)S(1)} %get-tuple-element., ...), custom_call_target="tpu_custom_call" | custom-call | tf_op jit(solution)/shard_map/pallas_call | solution.py:779
  (4 shorter events, 0.0 us)
Async XLA Ops:
  0.6 0.7 %copy-start.8 = (f32[1,512]{1,0:T(1,128)S(1)}, f32[1,512]{1,0:T(1,128)}, u32[]{:S(2)}) copy-start(f32[1,512]{1,0:T(1,128)} %refs_5_.1) | copy-start | bytes 6148
  0.7 0.7 %copy-start.11 = (f32[256]{0:T(256)S(1)}, f32[256]{0:T(256)}, u32[]{:S(2)}) copy-start(f32[256]{0:T(256)} %param.14) | copy-start | bytes 3076
  0.7 0.7 %copy-start.12 = (s32[8]{0:T(128)S(1)}, s32[8]{0:T(128)}, u32[]{:S(2)}) copy-start(s32[8]{0:T(128)} %refs_12_.1) | copy-start | bytes 100
  1.3 1.0 %copy-start = (bf16[256,1024]{1,0:T(8,128)(2,1)S(1)}, bf16[256,1024]{1,0:T(8,128)(2,1)}, u32[]{:S(2)}) copy-start(bf16[256,1024]{1,0:T(8,128)(2,1)} %refs_2_.1) | copy-start | bytes 1572868
  2.4 0.9 %copy-start.1 = (bf16[512,256]{1,0:T(8,128)(2,1)S(1)}, bf16[512,256]{1,0:T(8,128)(2,1)}, u32[]{:S(2)}) copy-start(bf16[512,256]{1,0:T(8,128)(2,1)} %refs_3_.1) | copy-start | bytes 786436
  3.3 0.8 %copy-start.2 = (bf16[128,256]{1,0:T(8,128)(2,1)S(1)}, bf16[128,256]{1,0:T(8,128)(2,1)}, u32[]{:S(2)}) copy-start(bf16[128,256]{1,0:T(8,128)(2,1)} %refs_0_.1) | copy-start | bytes 196612
  4.2 0.8 %copy-start.3 = (bf16[128,256]{1,0:T(8,128)(2,1)S(1)}, bf16[128,256]{1,0:T(8,128)(2,1)}, u32[]{:S(2)}) copy-start(bf16[128,256]{1,0:T(8,128)(2,1)} %refs_11_.1) | copy-start | bytes 196612
  5.0 0.8 %copy-start.4 = (bf16[1,512,48]{1,2,0:T(8,128)(2,1)S(1)}, bf16[1,512,48]{1,2,0:T(8,128)(2,1)}, u32[]{:S(2)}) copy-start(bf16[1,512,48]{1,2,0:T(8,128)(2,1)} %param.19) | copy-start | bytes 147460
  5.8 0.8 %copy-start.5 = (f32[1,16,512]{2,1,0:T(8,128)S(1)}, f32[1,16,512]{2,1,0:T(8,128)}, u32[]{:S(2)}) copy-start(f32[1,16,512]{2,1,0:T(8,128)} %refs_9_.1) | copy-start | bytes 98308
  6.6 0.7 %copy-start.6 = (bf16[1,16,512]{2,1,0:T(8,128)(2,1)S(1)}, bf16[1,16,512]{2,1,0:T(8,128)(2,1)}, u32[]{:S(2)}) copy-start(bf16[1,16,512]{2,1,0:T(8,128)(2,1)} %refs_7_.1) | copy-start | bytes 49156
  7.3 0.7 %copy-start.7 = (f32[1,4,512]{2,1,0:T(4,128)S(1)}, f32[1,4,512]{2,1,0:T(4,128)}, u32[]{:S(2)}) copy-start(f32[1,4,512]{2,1,0:T(4,128)} %refs_4_.1) | copy-start | bytes 24580
  8.0 0.7 %copy-start.9 = (f32[1,512]{1,0:T(1,128)S(1)}, f32[1,512]{1,0:T(1,128)}, u32[]{:S(2)}) copy-start(f32[1,512]{1,0:T(1,128)} %refs_8_.1) | copy-start | bytes 6148
  8.7 0.7 %copy-start.10 = (f32[1,512]{1,0:T(1,128)S(1)}, f32[1,512]{1,0:T(1,128)}, u32[]{:S(2)}) copy-start(f32[1,512]{1,0:T(1,128)} %refs_10_.1) | copy-start | bytes 6148

commit v2 on v1

--- a/solution.py
+++ b/solution.py
@@ -15,7 +15,6 @@
 RESET = 1e6
 HALO = 16
 LANES = 128
-GROUP = 16
 
 
 def dot(a, b, ca=1, cb=0):
@@ -30,8 +29,8 @@
     u = jnp.exp(-jnp.abs(v))
     s = u / (2.0 + u)
     q = s * s
-    p = 1.0 / 15.0
-    for k in (13.0, 11.0, 9.0, 7.0, 5.0, 3.0):
+    p = 1.0 / 13.0
+    for k in (11.0, 9.0, 7.0, 5.0, 3.0):
         p = p * q + 1.0 / k
     return jnp.maximum(v, 0.0) + 2.0 * s * (p * q + 1.0)
 
@@ -226,8 +225,8 @@
     (tok_h, gain_h, win_h, wout_h, cw_h, cb_h, wx_h, wdt_h, bias_h, alog_h, skip_h, cot_h, len_r,
      out_r, ing_r, etotal, esib, xtotal, xsib, ototal, gsib,
      tok_r, gain_r, win_r, wout_r, cw_r, cb_r, wx_r, wdt_r, bias_r, alog_r, skip_r, cot_r, lsem,
-     thalo, brep, crep, dref, hs, lamr, rar, sdr, sar, gyr, xpad, gpad, gext, ghsend, ghrecv,
-     xin1, xsend2, xin2, yr, mgr, mbr, adjr, dtar, bsend, brecv, vsend, vrecv,
+     thalo, picked, bcr, dref, hs, sdr, sar, gyr, xpad, gpad, gext, ghsend, ghrecv,
+     xin1, xsend2, xin2, yr, adjr, dtar, bsend, brecv, vsend, vrecv,
      epair, eprecv, epart, es1, er1, es2, er2, eb3,
      xpair, xprecv, xpart, xs1, xr1, xb3, opart, os1, or1, ob3,
      ssem, rsem) = refs
@@ -235,8 +234,6 @@
     inner = wout_r.shape[0]
     state = alog_r.shape[1]
     chunks = inner // LANES
-    groups = rows // GROUP
-    blk = GROUP * state
     dirn = lax.axis_index("dir")
     seq = lax.axis_index("seq")
     place = seq + dirn * (n - 1 - 2 * seq)
@@ -338,26 +335,32 @@
             conv = conv + jnp.where(dist_own[:count] >= k, tap, 0.0)
         sig_c = jax.nn.sigmoid(conv)
         act_b = (conv * sig_c).astype(B16)
-        px = dot(wx_r[0], act_b, 1, 1)
-        pre = dot(px[:state].astype(B16), wdt_r[0], 0, 0) + bias_r[...]
+        low_t = dot(wx_r[0, pl.ds(0, state)], act_b, 1, 1).astype(B16)
+        bc = dot(act_b, wx_r[0, pl.ds(state, 2 * state)], 1, 1)
+        pre = dot(low_t, wdt_r[0], 0, 0) + bias_r[...]
         step = softplus(pre)
         sd = jnp.where(dist_own[:count] == 0, RESET, step)
         sdr[pl.ds(0, count)] = sd
         sar[pl.ds(0, count)] = step * act_b.astype(F32)
-        return conv, sig_c, act_b, px, pre, step, sd
-
-    def spread(b_t, c_t, first, last):
-        def body(g, carry):
-            shift = lax.rem(LANES - g * 8, LANES)
-            br = pltpu.roll(b_t, shift, 1)
-            cr = pltpu.roll(c_t, shift, 1)
-            for j in range(8):
-                at = pl.ds(pl.multiple_of((g * 8 + j) * state, state), state)
-                brep[at] = jnp.broadcast_to(br[:, j:j + 1], (state, LANES))
-                crep[at] = jnp.broadcast_to(cr[:, j:j + 1], (state, LANES))
-            return carry
-
-        lax.fori_loop(first, last, body, 0)
+        return conv, sig_c, act_b, low_t, pre, step, sd, bc
+
+    wide = 2 * state
+    lane_k = lax.broadcasted_iota(jnp.int32, (state, LANES), 1)
+    row_k = lax.broadcasted_iota(jnp.int32, (state, LANES), 0)
+    own_k = jnp.where((lane_k < 2 * wide) & (lax.rem(lane_k, state) == row_k), 1.0, 0.0)
+    fan_r = lax.rem(lax.broadcasted_iota(jnp.int32, (LANES, 2 * LANES), 0), wide) // state
+    fan_c = lax.broadcasted_iota(jnp.int32, (LANES, 2 * LANES), 1) // LANES
+    fan = jnp.where(fan_r == fan_c, 1.0, 0.0).astype(B16)
+
+    def spread(bc, first):
+        count = bc.shape[0]
+        top = bc.astype(B16).astype(F32)
+        none = jnp.zeros((count, LANES - 2 * wide), F32)
+        both = jnp.concatenate([top, bc - top, none], axis=1)
+        for t in range(count):
+            picked[pl.ds((first + t) * state, state)] = (both[t:t + 1] * own_k).astype(B16)
+        at = pl.ds(first * state, count * state)
+        bcr[at] = dot(picked[at], fan)
 
     def summarise(g, carry):
         h, p, l = [list(x) for x in carry]
@@ -365,7 +368,7 @@
         sd8, sa8, gy8 = sdr[at8], sar[at8], gyr[at8]
         for j in range(8):
             at = pl.ds(pl.multiple_of((g * 8 + j) * state, state), state)
-            br, cr = brep[at], crep[at]
+            br, cr = bcr[at, :LANES], bcr[at, LANES:]
             for c in range(chunks):
                 lane = slice(c * LANES, (c + 1) * LANES)
                 d = jnp.exp2(sd8[j:j + 1, lane] * a2[c])
@@ -381,8 +384,8 @@
     head = HALO // 8
 
     whole = drive(rows)
-    spread(whole[3][state:2 * state], whole[3][2 * state:], head, rows // 8)
-    h_late, p_late, l_late = lax.fori_loop(head, rows // 8, summarise, (zero, one, zero))
+    spread(whole[7][HALO:], HALO)
+    h_late, p_late, l_late = lax.fori_loop(head, rows // 8, summarise, (zero, one, zero), unroll=1)
 
     @pl.when(place > 0)
     def _():
@@ -391,101 +394,105 @@
     _, vr_h, normed_h = normalise(turned(thalo[...], turn_h))
     xpad[pl.ds(0, HALO)] = dot(normed_h, win_r[:, :inner]).astype(B16).astype(F32)
     start = drive(HALO)
-    first_px = jnp.concatenate([start[3], jnp.zeros((start[3].shape[0], rows - HALO), F32)], axis=1)
-    lane_px = lax.broadcasted_iota(jnp.int32, first_px.shape, 1)
-    px = jnp.where(lane_px < HALO, first_px, whole[3])
+    low_first = jnp.concatenate([start[3].astype(F32), jnp.zeros((state, rows - HALO), F32)], axis=1)
+    lane_low = lax.broadcasted_iota(jnp.int32, low_first.shape, 1)
+    dt_low = jnp.where(lane_low < HALO, low_first, whole[3].astype(F32)).astype(B16)
     patch = lambda i: jnp.concatenate([start[i], whole[i][HALO:]], axis=0)
     conv, sig_c, act_b, pre, step, sd = [patch(i) for i in (0, 1, 2, 4, 5, 6)]
     act = act_b.astype(F32)
-    dt_low = px[:state].astype(B16)
-    b_t = px[state:2 * state]
-    c_t = px[2 * state:]
-    spread(b_t, c_t, 0, head)
+    spread(start[7], 0)
     h_first, p_first, l_first = lax.fori_loop(0, head, summarise, (zero, one, zero))
     h_sum = join(h_late) + join(p_late) * join(h_first)
     l_sum = join(l_first) + join(p_first) * join(l_late)
 
     def pair_rows(v):
-        top = v.astype(B16)
-        rest = (v - top.astype(F32)).astype(B16)
-        r = lax.broadcasted_iota(jnp.int32, (16, v.shape[1]), 0)
-        both = jnp.where(r == 0, top.astype(F32), jnp.where(r == 1, rest.astype(F32), 0.0))
-        return both.astype(B16)
-
-    unpair = lambda v: v[0:1].astype(F32) + v[1:2].astype(F32)
-    xin1[lo, pl.ds(0, state)] = h_sum.astype(B16)
-    xin1[lo, pl.ds(state, state)] = l_sum.astype(B16)
-    xin1[lo, pl.ds(2 * state, 16)] = pair_rows(jnp.sum(sd, axis=0, keepdims=True))
+        top = v.astype(B16).astype(F32)
+        both = cut(top) + cut(v - top) + [jnp.zeros((16 - 2 * chunks, LANES), F32)]
+        return jnp.concatenate(both, axis=0).astype(B16)
+
+    blk_s = chunks * state
+    stack = lambda v: jnp.concatenate(cut(v), axis=0).astype(B16)
+    unstack = lambda v, at: join([v[at + c * state:at + (c + 1) * state].astype(F32) for c in range(chunks)])
+    def unpair1(v):
+        r = v[blk_s:blk_s + 16].astype(F32)
+        return join([r[c:c + 1] + r[chunks + c:chunks + c + 1] for c in range(chunks)])
+    xin1[lo, pl.ds(0, blk_s)] = stack(h_sum)
+    xin1[lo, pl.ds(blk_s, 16)] = pair_rows(jnp.sum(sd, axis=0, keepdims=True))
+    xin1[lo, pl.ds(blk_s + 16, blk_s)] = stack(l_sum)
     ex1 = Exchange(ring, g_in, lo, lambda p: dev_at(hi * g_in + p))
     ex1.start(lambda p: xin1.at[lo], lambda s: xin1.at[s])
+
     ex1.wait()
-    sums = [unpair(xin1[j, pl.ds(2 * state, 16)]) for j in range(g_in)]
+    sums = [unpair1(xin1[j]) for j in range(g_in)]
     fwd = bwd = fwd_all = bwd_all = jnp.zeros((state, inner), F32)
     s_fwd = s_bwd = s_all = jnp.zeros((1, inner), F32)
     for j in range(g_in):
         fade = jnp.exp2(rate2 * sums[j])
-        fwd_all = fade * fwd_all + xin1[j, pl.ds(0, state)].astype(F32)
+        fwd_all = fade * fwd_all + unstack(xin1[j], 0)
         fwd = jnp.where(j < lo, fwd_all, fwd)
         s_all = s_all + sums[j]
         s_fwd = jnp.where(j < lo, s_all, s_fwd)
     for j in reversed(range(g_in)):
         fade = jnp.exp2(rate2 * sums[j])
-        bwd_all = fade * bwd_all + xin1[j, pl.ds(state, state)].astype(F32)
+        bwd_all = fade * bwd_all + unstack(xin1[j], blk_s + 16)
         bwd = jnp.where(j > lo, bwd_all, bwd)
         s_bwd = jnp.where(j > lo, s_bwd + sums[j], s_bwd)
     s_pair = pair_rows(s_all)
-    xsend2[0, pl.ds(0, state)] = fwd_all.astype(B16)
-    xsend2[0, pl.ds(state, 16)] = s_pair
-    xsend2[1, pl.ds(0, state)] = bwd_all.astype(B16)
-    xsend2[1, pl.ds(state, 16)] = s_pair
+    for k, v in enumerate((fwd_all, bwd_all)):
+        xsend2[k, pl.ds(0, blk_s)] = stack(v)
+        xsend2[k, pl.ds(blk_s, 16)] = s_pair
     xin2[hi] = jnp.zeros(xin2.shape[1:], B16)
     ex2 = Exchange(ring, g_out, hi, lambda p: dev_at(p * g_in + lo))
     ex2.start(lambda p: xsend2.at[jnp.where(p > hi, 0, 1)], lambda s: xin2.at[s])
     ex2.wait()
     h_in = l_in = jnp.zeros((state, inner), F32)
     for k in range(g_out):
-        new = jnp.exp2(rate2 * unpair(xin2[k, pl.ds(state, 16)])) * h_in
-        h_in = jnp.where(k < hi, new + xin2[k, pl.ds(0, state)].astype(F32), h_in)
+        new = jnp.exp2(rate2 * unpair1(xin2[k])) * h_in
+        h_in = jnp.where(k < hi, new + unstack(xin2[k], 0), h_in)
     for k in reversed(range(g_out)):
-        new = jnp.exp2(rate2 * unpair(xin2[k, pl.ds(state, 16)])) * l_in
-        l_in = jnp.where(k > hi, new + xin2[k, pl.ds(0, state)].astype(F32), l_in)
+        new = jnp.exp2(rate2 * unpair1(xin2[k])) * l_in
+        l_in = jnp.where(k > hi, new + unstack(xin2[k], 0), l_in)
     h_in = jnp.exp2(rate2 * s_fwd) * h_in + fwd
     l_in = jnp.exp2(rate2 * s_bwd) * l_in + bwd
 
+    sub = lax.broadcasted_iota(jnp.int32, (8, LANES), 0)
+    lane_at = lax.broadcasted_iota(jnp.int32, (state, LANES), 1)
+
+    def sum_rows(v):
+        for bit in (1, 2, 4):
+            mine = lax.rem(sub // bit, 2) == 0
+            v = [
+                jnp.where(mine, a, b) + pltpu.roll(jnp.where(mine, b, a), bit, 0)
+                for a, b in zip(v[::2], v[1::2])
+            ]
+        return v[0]
+
+    halve = lambda v: v[:8] + v[8:]
     hs[pl.ds(0, state)] = h_in
 
-    def forward(g, h):
-        h = list(h)
+    def forward(g, carry):
+        h, gc = list(carry[0]), carry[1]
         at8 = pl.ds(pl.multiple_of(g * 8, 8), 8)
-        sa8 = sar[at8]
+        sa8, gy8 = sar[at8], gyr[at8]
+        over = [None] * 8
+        for c in range(chunks):
+            lane = slice(c * LANES, (c + 1) * LANES)
+            ys = []
+            for j in range(8):
+                at = pl.ds(pl.multiple_of((g * 8 + j) * state, state), state)
+                nxt = pl.ds(pl.multiple_of((g * 8 + j + 1) * state, state), state)
+                h[c] = dref[at, lane] * h[c] + sa8[j:j + 1, lane] * bcr[at, :LANES]
+                hs[nxt, lane] = h[c]
+                ys.append(halve(h[c] * bcr[at, LANES:]))
+                new = h[c] * gy8[j:j + 1, lane]
+                over[j] = new if c == 0 else over[j] + new
+            yr[at8, lane] = sum_rows(ys)
         for j in range(8):
-            at = pl.ds(pl.multiple_of((g * 8 + j) * state, state), state)
-            nxt = pl.ds(pl.multiple_of((g * 8 + j + 1) * state, state), state)
-            br = brep[at]
-            for c in range(chunks):
-                lane = slice(c * LANES, (c + 1) * LANES)
-                h[c] = dref[at, lane] * h[c] + sa8[j:j + 1, lane] * br
-                hs[nxt, lane] = h[c]
-        return tuple(h)
-
-    lax.fori_loop(0, rows // 8, forward, tuple(cut(h_in)))
-
-    lane_n = lax.broadcasted_iota(jnp.int32, (state, blk), 1)
-    row_n = lax.broadcasted_iota(jnp.int32, (state, blk), 0)
-    rep = jnp.where(lax.rem(lane_n, state) == row_n, 1.0, 0.0).astype(B16)
-    lane_t = lax.broadcasted_iota(jnp.int32, (rows, blk), 1) // state
-    row_t = lax.rem(lax.broadcasted_iota(jnp.int32, (rows, blk), 0), GROUP)
-    on = lane_t == row_t
-    bdiag = jnp.where(on, dot(b_t.astype(B16), rep, 0, 0), 0.0).astype(B16)
-    cdiag = jnp.where(on, dot(c_t.astype(B16), rep, 0, 0), 0.0).astype(B16)
-    odiag = jnp.where(on, 1.0, 0.0).astype(B16)
-    gy_b = gy.astype(B16)
-    sa_b = (step * act).astype(B16)
-    for g in range(groups):
-        t = slice(g * GROUP, (g + 1) * GROUP)
-        xh = hs[pl.ds(g * blk + state, blk)].astype(B16)
-        yr[pl.ds(g * GROUP, GROUP)] = dot(cdiag[t], xh)
-        mgr[pl.ds(g * GROUP, GROUP)] = dot(gy_b[t], xh, 1, 1)
+            gc = jnp.where(lane_at == g * 8 + j, jnp.sum(over[j], axis=1, keepdims=True), gc)
+        return tuple(h), gc
+
+    none = jnp.zeros((state, rows), F32)
+    _, g_c = lax.fori_loop(0, rows // 8, forward, (tuple(cut(h_in)), none))
     y = yr[...] + skip_r[...] * act
     mixed = (y * gate).astype(B16)
     gz = (gmix * y * silu_grad(zgate, sig_z)).astype(B16)
@@ -508,45 +515,43 @@
     ring.sent.append(b_copy)
 
     def backward(i, carry):
-        m, acc = [list(x) for x in carry]
+        m, acc, gb = list(carry[0]), list(carry[1]), carry[2]
         g = rows // 8 - 1 - i
         at8 = pl.ds(pl.multiple_of(g * 8, 8), 8)
-        sd8, gy8 = sdr[at8], gyr[at8]
-        for j in reversed(range(8)):
-            at = pl.ds(pl.multiple_of((g * 8 + j) * state, state), state)
-            cr = crep[at]
-            for c in range(chunks):
-                lane = slice(c * LANES, (c + 1) * LANES)
-                lam = m[c] + gy8[j:j + 1, lane] * cr
-                lamr[at, lane] = lam
+        sd8, gy8, sa8 = sdr[at8], gyr[at8], sar[at8]
+        over = [None] * 8
+        for c in range(chunks):
+            lane = slice(c * LANES, (c + 1) * LANES)
+            adjs, dts = [None] * 8, [None] * 8
+            for j in reversed(range(8)):
+                at = pl.ds(pl.multiple_of((g * 8 + j) * state, state), state)
+                lam = m[c] + gy8[j:j + 1, lane] * bcr[at, LANES:]
                 m[c] = dref[at, lane] * lam
                 r = m[c] * hs[at, lane] * a1[c]
-                rar[at, lane] = r
                 acc[c] = acc[c] + r * sd8[j:j + 1, lane]
-        return tuple(m), tuple(acc)
-
-    _, galog = lax.fori_loop(0, rows // 8, backward, (tuple(cut(l_in)), zero))
-    galog = join(galog)
-
+                adjs[j] = halve(lam * bcr[at, :LANES])
+                dts[j] = halve(r)
+                new = lam * sa8[j:j + 1, lane]
+                over[j] = new if c == 0 else over[j] + new
+            adjr[at8, lane] = sum_rows(adjs)
+            dtar[at8, lane] = sum_rows(dts)
+        for j in range(8):
+            gb = jnp.where(lane_at == g * 8 + j, jnp.sum(over[j], axis=1, keepdims=True), gb)
+        return tuple(m), tuple(acc), gb
+
+    carry = lax.fori_loop(0, rows // 32, backward, (tuple(cut(l_in)), zero, none))
     early = Reduce(ring, n, seq, dirn, epart, etotal, es1, er1, es2, er2, eb3)
     e_copy.wait_recv()
     epart[...] = epart[...] + eprecv[...].astype(F32)
     early.scatter1()
-
-    for g in range(groups):
-        t = slice(g * GROUP, (g + 1) * GROUP)
-        at = pl.ds(g * blk, blk)
-        xl = lamr[at].astype(B16)
-        adjr[pl.ds(g * GROUP, GROUP)] = dot(bdiag[t], xl)
-        mbr[pl.ds(g * GROUP, GROUP)] = dot(sa_b[t], xl, 1, 1)
-        dtar[pl.ds(g * GROUP, GROUP)] = dot(odiag[t], rar[at].astype(B16))
+    _, galog, g_b = lax.fori_loop(rows // 32, rows // 8, backward, carry)
+    galog = join(galog)
     adj = adjr[...]
     gpre = (dtar[...] + adj * act) * jax.nn.sigmoid(pre)
     gbias = jnp.sum(gpre, axis=0, keepdims=True)
     gpre = gpre.astype(B16)
     gwdt = dot(dt_low, gpre)
-    sel = lambda m: dot(rep, jnp.where(on, m, 0.0).astype(B16), 1, 1)
-    gpx = jnp.concatenate([dot(wdt_r[0], gpre, 1, 1), sel(mbr[...]), sel(mgr[...])], axis=0).astype(B16)
+    gpx = jnp.concatenate([dot(wdt_r[0], gpre, 1, 1), g_b, g_c], axis=0).astype(B16)
     gwx_t = dot(gpx, act_b)
     gact = gy * skip_r[...] + adj * step + dot(gpx, wx_r[0], 0, 0)
     gconv_b = (gact * silu_grad(conv, sig_c)).astype(B16)
@@ -631,17 +636,12 @@
     v_copy = ring.copy(vsend, vrecv, bv, bv, sibling)
     v_copy.start()
     ring.sent.append(v_copy)
+    own.gather()
     early.gather2()
-    own.gather()
     xlate.gather()
-    early.gather1()
     v_copy.wait_recv()
     ing_r[...] = cot_r[...].astype(F32) + (vsend[...].astype(F32) + vrecv[...].astype(F32))
-    early.finish()
-    bs = ring.take(1)
-    es_copy = ring.copy(etotal, esib, bs, bs, sibling)
-    es_copy.start()
-    ring.sent.append(es_copy)
+    early.gather1()
     own.finish()
     bo = ring.take(1)
     gat = pl.ds(row - 16, 16)
@@ -653,6 +653,11 @@
     xs_copy = ring.copy(xtotal, xsib, bs2, bs2, sibling)
     xs_copy.start()
     ring.sent.append(xs_copy)
+    early.finish()
+    bs = ring.take(1)
+    es_copy = ring.copy(etotal, esib, bs, bs, sibling)
+    es_copy.start()
+    ring.sent.append(es_copy)
     es_copy.wait_recv()
     os_copy.wait_recv()
     xs_copy.wait_recv()
@@ -726,6 +731,7 @@
     g_in, g_out = log_split(n)
     g3 = max(n // 16, 1)
     hw = inner // 2
+    cells = state * inner // LANES
     gain = gain.reshape(1, width)
     w_xt = jnp.swapaxes(w_x, 1, 2)
     nsem = 16 + g_in + g_out + 16 + 4 * 16 + 3 * g3
@@ -736,16 +742,14 @@
     scratch = [vm(x.shape, x.dtype) for x in ins] + [
         pltpu.SemaphoreType.DMA((len(ins),)),
         vm((HALO, width), B16),
-        vm((rows * state, LANES), F32), vm((rows * state, LANES), F32),
+        vm((rows * state, LANES), B16), vm((rows * state, 2 * LANES), F32),
         vm((rows * state, inner), F32), vm(((rows + 1) * state, inner), F32),
-        vm((rows * state, inner), F32), vm((rows * state, inner), F32),
         vm((rows, inner), F32), vm((rows, inner), F32), vm((rows, inner), F32),
         vm((HALO + rows, inner), F32), vm((rows + HALO, inner), F32), vm((2 * HALO, inner), F32),
         vm((HALO, inner), B16), vm((HALO, inner), B16),
-        vm((g_in, 2 * state + 16, inner), B16), vm((2, state + 16, inner), B16),
-        vm((g_out, state + 16, inner), B16),
-        vm((rows, inner), F32), vm((rows, GROUP * state), F32), vm((rows, GROUP * state), F32),
-        vm((rows, inner), F32), vm((rows, inner), F32),
+        vm((g_in, 2 * cells + 16, LANES), B16), vm((2, cells + 16, LANES), B16),
+        vm((g_out, cells + 16, LANES), B16),
+        vm((rows, inner), F32), vm((rows, inner), F32), vm((rows, inner), F32),
         vm((rows, width), F32), vm((rows, width), F32),
         vm((rows, width), B16), vm((rows, width), B16),
         vm((2, width, inner), B16), vm((width, inner), B16), vm((width, inner), F32),
@@ -767,7 +771,7 @@
         out_specs=[in_vmem] * len(mids),
         scratch_shapes=scratch,
         compiler_params=pltpu.CompilerParams(
-            collective_id=0, has_side_effects=True, vmem_limit_bytes=40 * 2**20
+            collective_id=0, has_side_effects=True, vmem_limit_bytes=56 * 2**20
         ),
     )(*ins, lengths)
     outs = (

time: 59.8 us -> 49.6 us (0.83)
  local copies, waits for them, and re-layouts: 8.67 us -> 0 us
  Pallas kernels: 49.8 us -> 48.8 us
    unnamed x26 -> x0, local copies, waits for them, and re-layouts: 8.67 us -> none
    pallas_call x1, Pallas kernels: 48.5 us -> 47.4 us  [on_device(): pl.pallas_call(functools.partial(kernel, n, nsem), out_shape=mids, in_spe...]
where the time goes in v2:
time: 49.6 us; the launch traced here: 49.5 us
  Pallas kernels  48.8 us (98%)
  between operations  0.66 us (1%)
    pallas_call x1, Pallas kernels, on_device(): pl.pallas_call(functools.partial(kernel, n, nsem), out_shape=mids, in_spe...  47.4 us
    pallas_call x1, Pallas kernels, on_device(): pl.pallas_call(functools.partial(finish, (w_xt.shape[1], rank, state)), o...  1.38 us

profile of v2, /device:TPU:1, one launch (start us, length us, event | category | flops | bytes accessed | tf_op | source)
XLA Modules:
  0.0 49.5 jit_solution(13205595973524994538)
XLA Ops:
  0.6 47.4 %shard_map.220 = (bf16[128,256]{1,0:T(8,128)(2,1)S(1)}, f32[128,256]{1,0:T(8,128)S(1)}, bf16[256,512]{1,0:T(8,128)(2,1)S(1)}, bf16[256,512]{1,0:T(8,128)(2,1)S(1...) custom-call(bf16[128,256]{1,0:T(8,128)(2,1)} %refs_0_.1, ...), custom_call_target="tpu_custom_call" | custom-call | tf_op jit(solution)/shard_map/pallas_call | solution.py:767
  48.1 1.4 %shard_map.221 = (bf16[128,256]{1,0:T(8,128)(2,1)}, f32[128,256]{1,0:T(8,128)}, f32[1,256]{1,0:T(1,128)}, f32[256,1024]{1,0:T(8,128)}, f32[512,256]{1,0:T(8,128)...) custom-call(bf16[128,256]{1,0:T(8,128)(2,1)S(1)} %get-tuple-element., ...), custom_call_target="tpu_custom_call" | custom-call | tf_op jit(solution)/shard_map/pallas_call | solution.py:783

commit v3 on v2

--- a/solution.py
+++ b/solution.py
@@ -15,6 +15,7 @@
 RESET = 1e6
 HALO = 16
 LANES = 128
+E_TWO, X_TWO, O_TWO = (True, True, False), (True, False, False), (True, True, True)
 
 
 def dot(a, b, ca=1, cb=0):
@@ -73,163 +74,184 @@
             c.start()
             self.ring.sent.append(c)
 
+    def wait_one(self, r):
+        peer = lax.rem(self.me + r, self.size)
+        self.ring.copy(
+            self.src(peer), self.dst(peer), self.base + r, self.base + peer, self.dev(peer)
+        ).wait_recv()
+
     def wait(self):
         for r in range(1, self.size):
-            peer = lax.rem(self.me + r, self.size)
-            self.ring.copy(
-                self.src(peer), self.dst(peer), self.base + r, self.base + peer, self.dev(peer)
-            ).wait_recv()
-
-
-class Reduce:
-    def __init__(self, ring, n, seq, dirn, part, total, send1, recv1, send2, recv2, buf3):
-        g1, g2 = 4, 4
-        g3 = n // (g1 * g2)
-        self.g = (g1, g2, g3)
-        lo = lax.rem(seq, g1)
-        mid = lax.rem(seq // g1, g2)
-        hi = seq // (g1 * g2)
-        self.ids = (lo, mid, hi)
-        dev1 = lambda p: (dirn, seq - lo + p)
-        dev2 = lambda p: (dirn, seq + (p - mid) * g1)
-        dev3 = lambda p: (dirn, seq + (p - hi) * g1 * g2)
-        self.ex = [Exchange(ring, g1, lo, dev1), Exchange(ring, g2, mid, dev2)]
-        self.top = Exchange(ring, g3, hi, dev3) if g3 > 1 else None
-        self.back = [Exchange(ring, g2, mid, dev2), Exchange(ring, g1, lo, dev1)]
-        self.part, self.total = part, total
-        self.send1, self.recv1, self.send2, self.recv2, self.buf3 = send1, recv1, send2, recv2, buf3
-        self.q = part.shape[0] // g1
-        self.p = self.q // g2
-
-    def scatter1(self):
-        q = self.q
-        self.send1[...] = self.part[...].astype(B16)
-        self.ex[0].start(
-            lambda p: self.send1.at[pl.ds(pl.multiple_of(p * q, q), q)], lambda s: self.recv1.at[s]
-        )
-
-    def scatter2(self):
-        q, p_ = self.q, self.p
-        lo, mid, _ = self.ids
-        self.recv1[lo] = jnp.zeros(self.recv1.shape[1:], B16)
-        self.ex[0].wait()
-        acc = self.part[pl.ds(pl.multiple_of(lo * q, q), q)]
-        for j in range(self.g[0]):
-            acc = acc + self.recv1[j].astype(F32)
-        self.part[pl.ds(0, q)] = acc
-        self.send2[...] = acc.astype(B16)
-        self.ex[1].start(
-            lambda p: self.send2.at[pl.ds(pl.multiple_of(p * p_, p_), p_)],
-            lambda s: self.recv2.at[s],
-        )
-
-    def gather2(self):
-        q, p_ = self.q, self.p
-        lo, mid, hi = self.ids
-        self.recv2[mid] = jnp.zeros(self.recv2.shape[1:], B16)
-        self.ex[1].wait()
-        acc = self.part[pl.ds(pl.multiple_of(mid * p_, p_), p_)]
-        for j in range(self.g[1]):
-            acc = acc + self.recv2[j].astype(F32)
-        if self.top is not None:
-            self.buf3[hi] = acc.astype(B16)
-            self.top.start(lambda p: self.buf3.at[hi], lambda s: self.buf3.at[s])
-            self.top.wait()
-            acc = self.buf3[0].astype(F32)
-            for j in range(1, self.g[2]):
-                acc = acc + self.buf3[j].astype(F32)
-        at = lambda s: pl.ds(pl.multiple_of(lo * q + s * p_, p_), p_)
-        self.total[at(mid)] = acc.astype(B16)
-        self.back[0].start(lambda p: self.total.at[at(mid)], lambda s: self.total.at[at(s)])
-
-    def gather1(self):
-        q = self.q
-        lo = self.ids[0]
-        self.back[0].wait()
-        at = lambda s: pl.ds(pl.multiple_of(s * q, q), q)
-        self.back[1].start(lambda p: self.total.at[at(lo)], lambda s: self.total.at[at(s)])
-
-    def finish(self):
-        self.back[1].wait()
-
-
-class Direct:
-    def __init__(self, ring, n, seq, dirn, part, total, send, recv, buf3, pieces):
-        self.ring, self.part, self.total = ring, part, total
-        self.send, self.recv, self.buf3, self.pieces = send, recv, buf3, pieces
-        self.me, self.hi, self.g3 = lax.rem(seq, 16), seq // 16, n // 16
-        self.dev = lambda p: (dirn, seq - self.me + p)
-        self.s1, self.s2 = ring.take(16), ring.take(16)
-        self.top = Exchange(ring, self.g3, self.hi, lambda p: (dirn, seq + (p - self.hi) * 16)) if self.g3 > 1 else None
-        self.peers = [lax.rem(self.me + r, 16) for r in range(1, 16)]
-
-    def piece(self, p):
-        return lax.rem(p + 12, 16) if self.pieces < 16 else p
-
-    def at(self, p):
-        return pl.ds(pl.multiple_of(self.piece(p) * 16, 16), 16)
+            self.wait_one(r)
+
+
+def flip(a, mask):
+    for b in range(4):
+        if mask >> b & 1:
+            a = a + (1 << b) * (1 - 2 * lax.rem(a // (1 << b), 2))
+    return a
+
+
+class Sum:
+    def __init__(self, ring, n, seq, dirn, own, total, send, recv, over, blocks, two):
+        self.ring, self.own, self.total, self.send, self.over = ring, own, total, send, over
+        self.blocks, self.k, self.g3 = blocks, total.shape[0] // 16, n // 16
+        self.me, hi = lax.rem(seq, 16), seq // 16
+        self.hi = hi
+        base = seq - self.me
+        self.dev = lambda p: (dirn, base + p)
+        self.lo, self.mid = lax.rem(self.me, 4), self.me // 4
+        self.peers = [flip(self.me, m) for m in range(15, 0, -1)]
+        self.out_two, self.back_two, self.far_first = two
+        near = lambda p: self.dev(self.me - lax.rem(self.me, 4) + p)
+        far = lambda p: self.dev(p * 4 + lax.rem(self.me, 4))
+        if self.far_first:
+            near, far, self.lo, self.mid = far, near, self.mid, self.lo
+        if self.out_two:
+            self.recv, self.send2, self.recv2 = recv
+            self.ex1, self.ex2 = Exchange(ring, 4, self.lo, near), Exchange(ring, 4, self.mid, far)
+        else:
+            (self.recv,) = recv
+            self.s1 = ring.take(16)
+        if self.back_two:
+            self.back2, self.back1 = Exchange(ring, 4, self.mid, far), Exchange(ring, 4, self.lo, near)
+        else:
+            self.s2 = ring.take(16)
+        self.top = Exchange(ring, self.g3, hi, lambda p: (dirn, seq + (p - hi) * 16)) if self.g3 > 1 else None
+
+    def block(self, p):
+        if (self.out_two or self.back_two) and not self.far_first:
+            return lax.rem(p, 4) * 4 + p // 4
+        return p if self.blocks == 16 else lax.rem(p + 12, 16)
+
+    def at(self, b, count=1):
+        size = self.k * count
+        return pl.ds(pl.multiple_of(b * size, size), size)
 
     def owns(self, p, body):
-        if self.pieces < 16:
-            pl.when(self.piece(p) < self.pieces)(body)
+        if self.blocks < 16:
+            pl.when(self.block(p) < self.blocks)(body)
         else:
             body()
 
     def go(self, c, owner):
         self.owns(owner, c.start)
-        if self.pieces < 16:
-            self.ring.edges.append((c, self.piece(owner) < self.pieces))
+        if self.blocks < 16:
+            self.ring.edges.append((c, self.block(owner) < self.blocks))
         else:
             self.ring.sent.append(c)
 
     def scatter(self):
-        self.send[...] = self.part[...].astype(B16)
+        self.send[...] = self.own(slice(None)).astype(B16)
+        if self.out_two:
+            self.ex1.start(lambda p: self.send.at[self.at(p, 4)], lambda s: self.recv.at[s])
+            return
         for r, p in enumerate(self.peers):
-            c = self.ring.copy(self.send.at[self.at(p)], self.recv.at[self.me], self.s1 + r, self.s1 + self.me, self.dev(p))
-            self.go(c, p)
+            src = self.send.at[self.at(self.block(p))]
+            self.go(self.ring.copy(src, self.recv.at[self.me], self.s1 + r, self.s1 + self.me, self.dev(p)), p)
+
+    def scatter2(self):
+        self.recv[self.lo] = jnp.zeros(self.recv.shape[1:], B16)
+        self.ex1.wait()
+        acc = self.own(self.at(self.lo, 4))
+        for j in range(4):
+            acc = acc + self.recv[j].astype(F32)
+        self.send2[...] = acc.astype(B16)
+        self.ex2.start(lambda p: self.send2.at[self.at(p)], lambda s: self.recv2.at[s])
+
+    def add(self):
+        if self.out_two:
+            self.recv2[self.mid] = jnp.zeros(self.recv2.shape[1:], B16)
+            self.ex2.wait()
+            parts, count = self.recv2, 4
+            acc = self.send2[self.at(self.mid)].astype(F32)
+        else:
+            self.recv[self.me] = jnp.zeros(self.recv.shape[1:], B16)
+            for r, p in reversed(list(enumerate(self.peers))):
+                there = self.send.at[pl.ds(0, self.k)]
+                self.ring.copy(there, self.recv.at[p], self.s1 + r, self.s1 + p, self.dev(p)).wait_recv()
+            parts, count = self.recv, 16
+            acc = self.own(self.at(self.block(self.me)))
+        for j in range(count):
+            acc = acc + parts[j].astype(F32)
+        if self.top is not None:
+            self.over[self.hi] = acc.astype(B16)
+            self.top.start(lambda p: self.over.at[self.hi], lambda s: self.over.at[s])
+            self.top.wait()
+            for _ in range(1, self.g3):
+                self.ring.sent.pop().wait_send()
+            acc = self.over[0].astype(F32)
+            for j in range(1, self.g3):
+                acc = acc + self.over[j].astype(F32)
+        self.total[self.at(self.block(self.me))] = acc.astype(B16)
 
     def gather(self):
-        def add():
-            self.recv[self.me] = jnp.zeros(self.recv.shape[1:], B16)
-            for r, p in enumerate(self.peers):
-                self.ring.copy(
-                    self.send.at[pl.ds(0, 16)], self.recv.at[p], self.s1 + r, self.s1 + p, self.dev(p)
-                ).wait_recv()
-            acc = self.part[self.at(self.me)]
-            for j in range(16):
-                acc = acc + self.recv[j].astype(F32)
-            if self.top is not None:
-                self.buf3[self.hi] = acc.astype(B16)
-                self.top.start(lambda p: self.buf3.at[self.hi], lambda s: self.buf3.at[s])
-                self.top.wait()
-                for _ in range(1, self.g3):
-                    self.ring.sent.pop().wait_send()
-                acc = self.buf3[0].astype(F32)
-                for j in range(1, self.g3):
-                    acc = acc + self.buf3[j].astype(F32)
-            self.total[self.at(self.me)] = acc.astype(B16)
-
-        self.owns(self.me, add)
-        mine = self.total.at[self.at(self.me)]
+        self.owns(self.me, self.add)
+        mine = self.total.at[self.at(self.block(self.me))]
+        if self.back_two:
+            there = lambda s: self.total.at[self.at(self.lo * 4 + s)]
+            self.back2.start(lambda p: there(self.mid), there)
+            return
         for r, p in enumerate(self.peers):
             self.go(self.ring.copy(mine, mine, self.s2 + r, self.s2 + self.me, self.dev(p)), self.me)
 
+    def gather1(self):
+        self.back2.wait()
+        there = lambda s: self.total.at[self.at(s, 4)]
+        self.back1.start(lambda p: there(self.lo), there)
+
+    def took(self, p):
+        there = self.total.at[self.at(self.block(p))]
+        self.owns(p, self.ring.copy(there, there, self.s2, self.s2 + p, self.dev(p)).wait_recv)
+
     def finish(self):
-        for r, p in enumerate(self.peers):
-            there = self.total.at[self.at(p)]
-            c = self.ring.copy(there, there, self.s2 + r, self.s2 + p, self.dev(p))
-            self.owns(p, c.wait_recv)
+        for p in reversed(self.peers):
+            self.took(p)
+
+    def mirror(self, other, sibling):
+        copies = []
+
+        def on(quarter):
+            s = self.ring.take(1)
+            rows = self.at(quarter, 4)
+            c = self.ring.copy(self.total.at[rows], other.at[rows], s, s, sibling)
+            c.start()
+            self.ring.sent.append(c)
+            copies.append(c)
+
+        if self.back_two:
+            for r in range(4):
+                p = lax.rem(self.lo + r, 4)
+                if r > 0:
+                    self.back1.wait_one(r)
+                on(p)
+        else:
+            by_lo = self.out_two and not self.far_first
+            for r in range(4):
+                quarter = lax.rem((self.lo if by_lo else self.mid) + r, 4)
+                for x in range(4):
+                    other_at = lax.rem((self.mid if by_lo else self.lo) + x, 4)
+                    p = other_at * 4 + quarter if by_lo else quarter * 4 + other_at
+                    if r + x > 0:
+                        self.took(p)
+                on(quarter)
+        return copies
 
 
 def kernel(n, nsem, *refs):
     (tok_h, gain_h, win_h, wout_h, cw_h, cb_h, wx_h, wdt_h, bias_h, alog_h, skip_h, cot_h, len_r,
      out_r, ing_r, etotal, esib, xtotal, xsib, ototal, gsib,
      tok_r, gain_r, win_r, wout_r, cw_r, cb_r, wx_r, wdt_r, bias_r, alog_r, skip_r, cot_r, lsem,
-     thalo, picked, bcr, dref, hs, sdr, sar, gyr, xpad, gpad, gext, ghsend, ghrecv,
+     tail_s, halo, picked, bcr, dref, hs, sdr, sar, gyr, xpad, taps, later, gpad, gext, ghsend, ghrecv,
+     sgr, cgr, zgr, gsr, skr, ntx, woutf,
      xin1, xsend2, xin2, yr, adjr, dtar, bsend, brecv, vsend, vrecv,
-     epair, eprecv, epart, es1, er1, es2, er2, eb3,
-     xpair, xprecv, xpart, xs1, xr1, xb3, opart, os1, or1, ob3,
-     ssem, rsem) = refs
+     epair, eprecv, esend, *rest) = refs
+    erecv, rest = rest[:3 if E_TWO[0] else 1], rest[3 if E_TWO[0] else 1:]
+    eover, xpair, xprecv, xsend, *rest = rest
+    xrecv, rest = rest[:3 if X_TWO[0] else 1], rest[3 if X_TWO[0] else 1:]
+    xover, opart, osend, *rest = rest
+    orecv, rest = rest[:3 if O_TWO[0] else 1], rest[3 if O_TWO[0] else 1:]
+    oover, ssem, rsem = rest
     rows, width = tok_r.shape
     inner = wout_r.shape[0]
     state = alog_r.shape[1]
@@ -248,10 +270,15 @@
     down = lax.rem(place + n - 1, n)
 
     barrier = pltpu.get_barrier_semaphore()
-    s_lo, s_hi = lax.rem(seq, 16), seq // 16
-    peers = [sibling] + [(dirn, seq - s_lo + lax.rem(s_lo + r, 16)) for r in range(1, 16)]
+    line, s_hi = lax.rem(seq, 16), seq // 16
+    peers = [sibling, dev_at(up), dev_at(down)]
+    if all(E_TWO[:2] + X_TWO[:2] + O_TWO[:2]):
+        near, far = lax.rem(line, 4), line // 4
+        peers += [(dirn, seq - near + lax.rem(near + r, 4)) for r in range(1, 4)]
+        peers += [(dirn, seq + (lax.rem(far + r, 4) - far) * 4) for r in range(1, 4)]
+    else:
+        peers += [(dirn, seq - line + lax.rem(line + r, 16)) for r in range(1, 16)]
     if n != 16:
-        peers += [dev_at(up), dev_at(down)]
         peers += [(dirn, seq + (lax.rem(s_hi + r, n // 16) - s_hi) * 16) for r in range(1, n // 16)]
         peers += [dev_at(hi * g_in + lax.rem(lo + r, g_in)) for r in range(1, g_in)]
         peers += [dev_at(lax.rem(hi + r, g_out) * g_in + lo) for r in range(1, g_out)]
@@ -270,7 +297,7 @@
         c = lax.broadcasted_iota(jnp.int32, (size, size), 1)
         return jnp.where(c == r + dirn * (size - 1 - 2 * r), 1.0, 0.0).astype(B16)
 
-    turn_t, turn_f, turn_h = turn(rows), turn(width), turn(HALO)
+    turn_t, turn_f = turn(rows), turn(width)
     turned = lambda v, tt: dot(dot(tt, v).astype(B16), turn_f)
 
     total = n * rows
@@ -282,9 +309,10 @@
         delta = q - (before + dirn * (total - after - before))
         dist = jnp.where((delta >= 0) & (delta < dist), delta, dist)
         before = after
-    dist = jnp.concatenate([dist] * chunks, axis=1)
-    q_all = jnp.concatenate([q] * chunks, axis=1)
-    dist_own = dist[HALO:HALO + rows]
+    over_lanes = lambda v: jnp.concatenate([v] * (inner // v.shape[1]), axis=1)
+    for k in range(1, 4):
+        later[k - 1] = jnp.where((dist >= k) & (q < total), 1.0, 0.0)
+    dist_own = over_lanes(dist[HALO:HALO + rows])
 
     def normalise(v):
         inv = lax.rsqrt(jnp.mean(v * v, axis=1, keepdims=True) + NORM_EPS)
@@ -293,17 +321,20 @@
 
     for i in range(3):
         loads[i].wait()
-    inv, vr, normed = normalise(turned(tok_r[...], turn_t))
+    tok = turned(tok_r[...], turn_t)
+    inv, vr, normed = normalise(tok)
     proj = dot(normed, win_r[...])
-    xi = proj[:, :inner].astype(B16).astype(F32)
+    xi_b = proj[:, :inner].astype(B16)
+    xi = xi_b.astype(F32)
     zgate = proj[:, inner:]
     xpad[pl.ds(0, HALO)] = jnp.zeros((HALO, inner), F32)
     xpad[pl.ds(HALO, rows)] = xi
+    tail_s[:, :inner] = xi_b[rows - HALO:]
+    tail_s[:, inner:] = tok[rows - HALO:].astype(B16)
 
     pl.semaphore_wait(barrier, len(peers))
-    edge = pl.multiple_of((1 - dirn) * (rows - HALO), HALO)
     b0 = ring.take(1)
-    tok_copy = ring.copy(tok_r.at[pl.ds(edge, HALO)], thalo, b0, b0, dev_at(up))
+    tok_copy = ring.copy(tail_s, halo, b0, b0, dev_at(up))
     ring.edges.append((tok_copy, place < n - 1))
 
     @pl.when(place < n - 1)
@@ -312,7 +343,7 @@
 
     @pl.when(place == 0)
     def _():
-        thalo[...] = jnp.zeros(thalo.shape, B16)
+        halo[...] = jnp.zeros(halo.shape, B16)
 
     for i in range(3, len(pairs)):
         loads[i].wait()
@@ -329,10 +360,11 @@
     a1 = cut(rate)
 
     def drive(count):
-        conv = jnp.zeros((count, inner), F32) + cb_r[...]
-        for k in range(4):
-            tap = xpad[pl.ds(HALO - k, count)] * cw_r[0, k:k + 1]
-            conv = conv + jnp.where(dist_own[:count] >= k, tap, 0.0)
+        conv = xpad[pl.ds(HALO, count)] * cw_r[0, 0:1] + cb_r[...]
+        for k in range(1, 4):
+            tap = jnp.where(dist_own[:count] >= k, xpad[pl.ds(HALO - k, count)], 0.0)
+            taps[k - 1, pl.ds(0, count)] = tap
+            conv = conv + tap * cw_r[0, k:k + 1]
         sig_c = jax.nn.sigmoid(conv)
         act_b = (conv * sig_c).astype(B16)
         low_t = dot(wx_r[0, pl.ds(0, state)], act_b, 1, 1).astype(B16)
@@ -366,11 +398,11 @@
         h, p, l = [list(x) for x in carry]
         at8 = pl.ds(pl.multiple_of(g * 8, 8), 8)
         sd8, sa8, gy8 = sdr[at8], sar[at8], gyr[at8]
-        for j in range(8):
-            at = pl.ds(pl.multiple_of((g * 8 + j) * state, state), state)
-            br, cr = bcr[at, :LANES], bcr[at, LANES:]
-            for c in range(chunks):
-                lane = slice(c * LANES, (c + 1) * LANES)
+        for c in range(chunks):
+            lane = slice(c * LANES, (c + 1) * LANES)
+            for j in range(8):
+                at = pl.ds(pl.multiple_of((g * 8 + j) * state, state), state)
+                br, cr = bcr[at, :LANES], bcr[at, LANES:]
                 d = jnp.exp2(sd8[j:j + 1, lane] * a2[c])
                 dref[at, lane] = d
                 h[c] = d * h[c] + sa8[j:j + 1, lane] * br
@@ -385,14 +417,13 @@
 
     whole = drive(rows)
     spread(whole[7][HALO:], HALO)
-    h_late, p_late, l_late = lax.fori_loop(head, rows // 8, summarise, (zero, one, zero), unroll=1)
+    h_late, p_late, l_late = lax.fori_loop(head, rows // 8, summarise, (zero, one, zero), unroll=2)
 
     @pl.when(place > 0)
     def _():
         tok_copy.wait_recv()
 
-    _, vr_h, normed_h = normalise(turned(thalo[...], turn_h))
-    xpad[pl.ds(0, HALO)] = dot(normed_h, win_r[:, :inner]).astype(B16).astype(F32)
+    xpad[pl.ds(0, HALO)] = halo[:, :inner].astype(F32)
     start = drive(HALO)
     low_first = jnp.concatenate([start[3].astype(F32), jnp.zeros((state, rows - HALO), F32)], axis=1)
     lane_low = lax.broadcasted_iota(jnp.int32, low_first.shape, 1)
@@ -401,7 +432,7 @@
     conv, sig_c, act_b, pre, step, sd = [patch(i) for i in (0, 1, 2, 4, 5, 6)]
     act = act_b.astype(F32)
     spread(start[7], 0)
-    h_first, p_first, l_first = lax.fori_loop(0, head, summarise, (zero, one, zero))
+    h_first, p_first, l_first = lax.fori_loop(0, head, summarise, (zero, one, zero), unroll=2)
     h_sum = join(h_late) + join(p_late) * join(h_first)
     l_sum = join(l_first) + join(p_first) * join(l_late)
 
@@ -421,6 +452,16 @@
     xin1[lo, pl.ds(blk_s + 16, blk_s)] = stack(l_sum)
     ex1 = Exchange(ring, g_in, lo, lambda p: dev_at(hi * g_in + p))
     ex1.start(lambda p: xin1.at[lo], lambda s: xin1.at[s])
+
+    _, vr_h, normed_h = normalise(halo[:, inner:].astype(F32))
+    ntx[...] = jnp.concatenate([normed, normed_h], axis=0).T
+    sgr[...] = jax.nn.sigmoid(pre)
+    cgr[...] = silu_grad(conv, sig_c)
+    zgr[...] = gmix * silu_grad(zgate, sig_z)
+    gsr[...] = gy * skip_r[...]
+    skr[...] = skip_r[...] * act
+    woutf[...] = dot(wout_r[...], turn_f).astype(B16)
+    gskip = jnp.sum(gy * act, axis=0, keepdims=True)
 
     ex1.wait()
     sums = [unpair1(xin1[j]) for j in range(g_in)]
@@ -492,27 +533,19 @@
         return tuple(h), gc
 
     none = jnp.zeros((state, rows), F32)
-    _, g_c = lax.fori_loop(0, rows // 8, forward, (tuple(cut(h_in)), none))
-    y = yr[...] + skip_r[...] * act
+    _, g_c = lax.fori_loop(0, rows // 8, forward, (tuple(cut(h_in)), none), unroll=4)
+    y = yr[...] + skr[...]
     mixed = (y * gate).astype(B16)
-    gz = (gmix * y * silu_grad(zgate, sig_z)).astype(B16)
-    gskip = jnp.sum(gy * act, axis=0, keepdims=True)
-
-    gwz = dot(normed, gz, 0, 0)
-    gwo = dot(mixed, cot, 0, 0)
-    gwo = jnp.concatenate([gwo[:width], gwo[width:]], axis=1)
-    epair[0] = gwz.astype(B16)
-    epair[1] = gwo.astype(B16)
-    epart[...] = jnp.where(dirn == 0, gwz, gwo)
+    gz = (zgr[...] * y).astype(B16)
+
+    epair[0] = dot(ntx[:, :rows], gz).astype(B16)
+    gwo = dot(mixed, cot, 0, 0).astype(B16)
+    epair[1, :, :width] = gwo[:width]
+    epair[1, :, width:] = gwo[width:]
     be = ring.take(1)
     e_copy = ring.copy(epair.at[1 - dirn], eprecv, be, be, sibling)
     e_copy.start()
     ring.sent.append(e_copy)
-    bsend[...] = dot(dot(turn_t, mixed).astype(B16), dot(wout_r[...], turn_f).astype(B16))
-    bb = ring.take(1)
-    b_copy = ring.copy(bsend, brecv, bb, bb, sibling)
-    b_copy.start()
-    ring.sent.append(b_copy)
 
     def backward(i, carry):
         m, acc, gb = list(carry[0]), list(carry[1]), carry[2]
@@ -539,48 +572,43 @@
             gb = jnp.where(lane_at == g * 8 + j, jnp.sum(over[j], axis=1, keepdims=True), gb)
         return tuple(m), tuple(acc), gb
 
-    carry = lax.fori_loop(0, rows // 32, backward, (tuple(cut(l_in)), zero, none))
-    early = Reduce(ring, n, seq, dirn, epart, etotal, es1, er1, es2, er2, eb3)
+    carry = lax.fori_loop(0, rows // 32, backward, (tuple(cut(l_in)), zero, none), unroll=4)
+    e_own = lambda at: epair[dirn, at].astype(F32) + eprecv[at].astype(F32)
+    early = Sum(ring, n, seq, dirn, e_own, etotal, esend, erecv, eover, 16, E_TWO)
     e_copy.wait_recv()
-    epart[...] = epart[...] + eprecv[...].astype(F32)
-    early.scatter1()
-    _, galog, g_b = lax.fori_loop(rows // 32, rows // 8, backward, carry)
+    early.scatter()
+    _, galog, g_b = lax.fori_loop(rows // 32, rows // 8, backward, carry, unroll=4)
     galog = join(galog)
     adj = adjr[...]
-    gpre = (dtar[...] + adj * act) * jax.nn.sigmoid(pre)
+    gpre = (dtar[...] + adj * act) * sgr[...]
     gbias = jnp.sum(gpre, axis=0, keepdims=True)
     gpre = gpre.astype(B16)
-    gwdt = dot(dt_low, gpre)
-    gpx = jnp.concatenate([dot(wdt_r[0], gpre, 1, 1), g_b, g_c], axis=0).astype(B16)
-    gwx_t = dot(gpx, act_b)
-    gact = gy * skip_r[...] + adj * step + dot(gpx, wx_r[0], 0, 0)
-    gconv_b = (gact * silu_grad(conv, sig_c)).astype(B16)
+    glow = dot(gpre, wdt_r[0], 1, 1).astype(B16)
+    gbc = jnp.concatenate([g_b, g_c], axis=0).astype(B16)
+    gact = gsr[...] + adj * step + dot(gbc, wx_r[0, pl.ds(state, 2 * state)], 0, 0)
+    gact = gact + dot(glow, wx_r[0, pl.ds(0, state)])
+    gconv_b = (gact * cgr[...]).astype(B16)
     gconv = gconv_b.astype(F32)
 
     gpad[pl.ds(0, rows)] = gconv
     gpad[pl.ds(rows, HALO)] = jnp.zeros((HALO, inner), F32)
     gext[pl.ds(0, HALO)] = jnp.zeros((HALO, inner), F32)
     gext[pl.ds(HALO, HALO)] = gconv[:HALO]
-    gxi = jnp.zeros((rows, inner), F32)
+    gxi = gconv * cw_r[0, 0:1]
     gxe = jnp.zeros((HALO, inner), F32)
-    for k in range(4):
+    for k in range(1, 4):
         w = cw_r[0, k:k + 1]
-        gxi = gxi + jnp.where(dist[HALO + k:HALO + k + rows] >= k, gpad[pl.ds(k, rows)] * w, 0.0)
-        if k > 0:
-            gxe = gxe + jnp.where(dist[k:k + HALO] >= k, gext[pl.ds(k, HALO)] * w, 0.0)
-    gxi_b = jnp.concatenate([gxe, gxi], axis=0).astype(B16)
-    normed_x = jnp.concatenate([normed_h, normed], axis=0)
-    vr_x = jnp.concatenate([vr_h, vr], axis=0)
-    gwx_half = dot(normed_x, gxi_b, 0, 0)
+        gxi = gxi + gpad[pl.ds(k, rows)] * over_lanes(later[k - 1, pl.ds(HALO + k, rows)]) * w
+        gxe = gxe + gext[pl.ds(k, HALO)] * over_lanes(later[k - 1, pl.ds(k, HALO)]) * w
+    gxi_b = jnp.concatenate([gxi, gxe], axis=0).astype(B16)
+    gwx_half = dot(ntx[...], gxi_b).astype(B16)
     hw = inner // 2
-    left, right = gwx_half[:, :hw], gwx_half[:, hw:]
-    xpair[0] = left.astype(B16)
-    xpair[1] = right.astype(B16)
+    xpair[0] = gwx_half[:, :hw]
+    xpair[1] = gwx_half[:, hw:]
     bx = ring.take(1)
     x_copy = ring.copy(xpair.at[1 - dirn], xprecv, bx, bx, sibling)
     x_copy.start()
     ring.sent.append(x_copy)
-    xpart[...] = jnp.where(dirn == 0, left, right)
     ghsend[...] = gconv_b[:HALO]
     bh = ring.take(1)
     h_copy = ring.copy(ghsend, ghrecv, bh, bh, dev_at(down))
@@ -590,14 +618,14 @@
     def _():
         h_copy.start()
 
+    gwx_t = jnp.concatenate([dot(glow, act_b, 0, 0), dot(gbc, act_b)], axis=0)
+    gwdt = dot(dt_low, gpre)
     gn_x = dot(gxi_b, win_r[:, :inner], 1, 1)
     gn_z = dot(gz, win_r[:, inner:], 1, 1)
-    ggain = jnp.sum(gn_x * vr_x, axis=0, keepdims=True) + jnp.sum(gn_z * vr, axis=0, keepdims=True)
+    ggain = jnp.sum((gn_x[:rows] + gn_z) * vr, axis=0, keepdims=True)
+    ggain = ggain + jnp.sum(gn_x[rows:] * vr_h, axis=0, keepdims=True)
     gcb = jnp.sum(gconv, axis=0, keepdims=True)
-    gcw = [
-        jnp.sum(jnp.where(dist_own >= k, gconv * xpad[pl.ds(HALO - k, rows)], 0.0), axis=0, keepdims=True)
-        for k in range(4)
-    ]
+    gcw = [jnp.sum(gconv * (xi if k == 0 else taps[k - 1]), axis=0, keepdims=True) for k in range(4)]
     pad_gain = jnp.concatenate([ggain, jnp.zeros((1, inner - width), F32)], axis=1)
     tail = jnp.concatenate(gcw + [gcb, gbias, gskip, pad_gain], axis=0)
     row = 0
@@ -607,28 +635,31 @@
         opart[pl.ds(row + k, k)] = part[:, hw:]
         row += 2 * k
     opart[pl.ds(row, opart.shape[0] - row)] = jnp.zeros((opart.shape[0] - row, hw), F32)
-    own = Direct(ring, n, seq, dirn, opart, ototal, os1, or1, ob3, -(-row // 16))
+    own = Sum(ring, n, seq, dirn, lambda at: opart[at], ototal, osend, orecv, oover, 16 if any(O_TWO[:2]) else -(-row // 16), O_TWO)
     own.scatter()
-    xlate = Direct(ring, n, seq, dirn, xpart, xtotal, xs1, xr1, xb3, 16)
+    x_own = lambda at: xpair[dirn, at].astype(F32) + xprecv[at].astype(F32)
+    xlate = Sum(ring, n, seq, dirn, x_own, xtotal, xsend, xrecv, xover, 16, X_TWO)
     x_copy.wait_recv()
-    xpart[...] = xpart[...] + xprecv[...].astype(F32)
     xlate.scatter()
-    early.scatter2()
-    b_copy.wait_recv()
-    out_r[...] = (tok_r[...].astype(F32) + (bsend[...] + brecv[...])).astype(B16)
+    if E_TWO[0]:
+        early.scatter2()
+    bsend[...] = dot(dot(turn_t, mixed).astype(B16), woutf[...])
+    bb = ring.take(1)
+    b_copy = ring.copy(bsend, brecv, bb, bb, sibling)
+    b_copy.start()
+    ring.sent.append(b_copy)
 
     @pl.when(place < n - 1)
     def _():
         h_copy.wait_recv()
         gpad[pl.ds(rows, HALO)] = ghrecv[...].astype(F32)
 
-    edge_x = jnp.zeros((HALO, inner), F32)
-    for k in range(4):
-        at = HALO + rows - HALO + k
-        ok = (dist[at:at + HALO] >= k) & (q_all[at:at + HALO] < total)
-        edge_x = edge_x + jnp.where(ok, gpad[pl.ds(rows - HALO + k, HALO)] * cw_r[0, k:k + 1], 0.0)
+    edge_x = gpad[pl.ds(rows - HALO, HALO)] * cw_r[0, 0:1]
+    for k in range(1, 4):
+        ok = over_lanes(later[k - 1, pl.ds(rows + k, HALO)])
+        edge_x = edge_x + gpad[pl.ds(rows - HALO + k, HALO)] * ok * cw_r[0, k:k + 1]
     gn_edge = dot(edge_x.astype(B16), win_r[:, :inner], 1, 1)
-    gn = jnp.concatenate([gn_x[HALO:rows], gn_edge], axis=0) + gn_z
+    gn = jnp.concatenate([gn_x[:rows - HALO], gn_edge], axis=0) + gn_z
     scaled = gn * gain_r[...]
     gv = inv * (scaled - vr * jnp.mean(scaled * vr, axis=1, keepdims=True))
     vsend[...] = turned(gv.astype(B16), turn_t).astype(B16)
@@ -636,31 +667,38 @@
     v_copy = ring.copy(vsend, vrecv, bv, bv, sibling)
     v_copy.start()
     ring.sent.append(v_copy)
+    if not E_TWO[0]:
+        early.gather()
+    for v, two in ((own, O_TWO), (xlate, X_TWO)):
+        if two[0]:
+            v.scatter2()
+    if E_TWO[0] and (X_TWO[0] or O_TWO[0]):
+        early.gather()
     own.gather()
-    early.gather2()
+    if E_TWO[0] and not (X_TWO[0] or O_TWO[0]):
+        early.gather()
     xlate.gather()
+    b_copy.wait_recv()
+    out_r[...] = (tok_r[...].astype(F32) + (bsend[...] + brecv[...])).astype(B16)
     v_copy.wait_recv()
     ing_r[...] = cot_r[...].astype(F32) + (vsend[...].astype(F32) + vrecv[...].astype(F32))
-    early.gather1()
-    own.finish()
+    for v, two in ((early, E_TWO), (own, O_TWO), (xlate, X_TWO)):
+        if two[1]:
+            v.gather1()
+    if O_TWO[1]:
+        own.back1.wait()
+    else:
+        own.finish()
     bo = ring.take(1)
     gat = pl.ds(row - 16, 16)
     os_copy = ring.copy(ototal.at[gat], gsib, bo, bo, sibling)
     os_copy.start()
     ring.sent.append(os_copy)
-    xlate.finish()
-    bs2 = ring.take(1)
-    xs_copy = ring.copy(xtotal, xsib, bs2, bs2, sibling)
-    xs_copy.start()
-    ring.sent.append(xs_copy)
-    early.finish()
-    bs = ring.take(1)
-    es_copy = ring.copy(etotal, esib, bs, bs, sibling)
-    es_copy.start()
-    ring.sent.append(es_copy)
-    es_copy.wait_recv()
+    copies = xlate.mirror(xsib, sibling)
+    copies += early.mirror(esib, sibling)
+    for c in copies:
+        c.wait_recv()
     os_copy.wait_recv()
-    xs_copy.wait_recv()
     done_edges(ring)
     for c in ring.sent:
         c.wait_send()
@@ -734,28 +772,35 @@
     cells = state * inner // LANES
     gain = gain.reshape(1, width)
     w_xt = jnp.swapaxes(w_x, 1, 2)
-    nsem = 16 + g_in + g_out + 16 + 4 * 16 + 3 * g3
+    nsem = 24 + g_in + g_out + 3 * 32 + 3 * g3
     vm = pltpu.VMEM
     sds = jax.ShapeDtypeStruct
     ins = (tokens, gain, w_in, w_out, conv_w, conv_b, w_xt, w_dt, dt_bias, a_log, d_skip, cotangent)
-    direct = [vm((256, hw), F32), vm((256, hw), B16), vm((16, 16, hw), B16), vm((g3, 16, hw), B16)]
+    def bufs(two, k, lanes):
+        if two[0]:
+            return [vm((4, 4 * k, lanes), B16), vm((4 * k, lanes), B16), vm((4, k, lanes), B16)]
+        return [vm((16, k, lanes), B16)]
+
+    k = width // 16
     scratch = [vm(x.shape, x.dtype) for x in ins] + [
         pltpu.SemaphoreType.DMA((len(ins),)),
-        vm((HALO, width), B16),
+        vm((HALO, inner + width), B16), vm((HALO, inner + width), B16),
         vm((rows * state, LANES), B16), vm((rows * state, 2 * LANES), F32),
         vm((rows * state, inner), F32), vm(((rows + 1) * state, inner), F32),
         vm((rows, inner), F32), vm((rows, inner), F32), vm((rows, inner), F32),
-        vm((HALO + rows, inner), F32), vm((rows + HALO, inner), F32), vm((2 * HALO, inner), F32),
+        vm((HALO + rows, inner), F32), vm((3, rows, inner), F32), vm((3, rows + 2 * HALO, LANES), F32),
+        vm((rows + HALO, inner), F32), vm((2 * HALO, inner), F32),
         vm((HALO, inner), B16), vm((HALO, inner), B16),
+        *[vm((rows, inner), F32)] * 5, vm((width, rows + HALO), B16), vm((inner, width), B16),
         vm((g_in, 2 * cells + 16, LANES), B16), vm((2, cells + 16, LANES), B16),
         vm((g_out, cells + 16, LANES), B16),
         vm((rows, inner), F32), vm((rows, inner), F32), vm((rows, inner), F32),
         vm((rows, width), F32), vm((rows, width), F32),
         vm((rows, width), B16), vm((rows, width), B16),
-        vm((2, width, inner), B16), vm((width, inner), B16), vm((width, inner), F32),
-        vm((width, inner), B16), vm((4, width // 4, inner), B16),
-        vm((width // 4, inner), B16), vm((4, width // 16, inner), B16), vm((g3, width // 16, inner), B16),
-        vm((2, width, hw), B16), vm((width, hw), B16), *direct, *direct,
+        vm((2, width, inner), B16), vm((width, inner), B16), vm((width, inner), B16), *bufs(E_TWO, k, inner), vm((g3, k, inner), B16),
+        vm((2, width, hw), B16), vm((width, hw), B16),
+        vm((width, hw), B16), *bufs(X_TWO, k, hw), vm((g3, k, hw), B16),
+        vm((256, hw), F32), vm((256, hw), B16), *bufs(O_TWO, 16, hw), vm((g3, 16, hw), B16),
         pltpu.SemaphoreType.DMA((nsem,)), pltpu.SemaphoreType.DMA((nsem,)),
     ]
     mids = [

time: 49.6 us -> 45.3 us (0.913)
  Pallas kernels: 48.8 us -> 44.5 us
    pallas_call x1, Pallas kernels: 47.4 us -> 43.1 us  [on_device(): pl.pallas_call(functools.partial(kernel, n, nsem), out_shape=mids, in_spe...]
where the time goes in v3:
time: 45.3 us; the launch traced here: 45.1 us
  Pallas kernels  44.5 us (98%)
  between operations  0.66 us (1%)
    pallas_call x1, Pallas kernels, on_device(): pl.pallas_call(functools.partial(kernel, n, nsem), out_shape=mids, in_spe...  43.1 us
    pallas_call x1, Pallas kernels, on_device(): pl.pallas_call(functools.partial(finish, (w_xt.shape[1], rank, state)), o...  1.38 us

profile of v3, /device:TPU:1, one launch (start us, length us, event | category | flops | bytes accessed | tf_op | source)
XLA Modules:
  0.0 45.1 jit_solution(5401077454350393980)
XLA Ops:
  0.6 43.1 %shard_map.220 = (bf16[128,256]{1,0:T(8,128)(2,1)S(1)}, f32[128,256]{1,0:T(8,128)S(1)}, bf16[256,512]{1,0:T(8,128)(2,1)S(1)}, bf16[256,512]{1,0:T(8,128)(2,1)S(1...) custom-call(bf16[128,256]{1,0:T(8,128)(2,1)} %refs_0_.1, ...), custom_call_target="tpu_custom_call" | custom-call | tf_op jit(solution)/shard_map/pallas_call | solution.py:812
  43.7 1.4 %shard_map.221 = (bf16[128,256]{1,0:T(8,128)(2,1)}, f32[128,256]{1,0:T(8,128)}, f32[1,256]{1,0:T(1,128)}, f32[256,1024]{1,0:T(8,128)}, f32[512,256]{1,0:T(8,128)...) custom-call(bf16[128,256]{1,0:T(8,128)(2,1)S(1)} %get-tuple-element., ...), custom_call_target="tpu_custom_call" | custom-call | tf_op jit(solution)/shard_map/pallas_call | solution.py:828

commit v4 on v3

--- a/solution.py
+++ b/solution.py
@@ -242,8 +242,8 @@
     (tok_h, gain_h, win_h, wout_h, cw_h, cb_h, wx_h, wdt_h, bias_h, alog_h, skip_h, cot_h, len_r,
      out_r, ing_r, etotal, esib, xtotal, xsib, ototal, gsib,
      tok_r, gain_r, win_r, wout_r, cw_r, cb_r, wx_r, wdt_r, bias_r, alog_r, skip_r, cot_r, lsem,
-     tail_s, halo, picked, bcr, dref, hs, sdr, sar, gyr, xpad, taps, later, gpad, gext, ghsend, ghrecv,
-     sgr, cgr, zgr, gsr, skr, ntx, woutf,
+     tail_s, halo, picked, bcr, dref, cpr, hs, pr, sdr, sar, gyr, xpad, taps, later, gpad, gext, ghsend, ghrecv,
+     sgr, cgr, zgr, gsr, skr, gyq, yl, ntx, woutf,
      xin1, xsend2, xin2, yr, adjr, dtar, bsend, brecv, vsend, vrecv,
      epair, eprecv, esend, *rest) = refs
     erecv, rest = rest[:3 if E_TWO[0] else 1], rest[3 if E_TWO[0] else 1:]
@@ -363,7 +363,6 @@
         conv = xpad[pl.ds(HALO, count)] * cw_r[0, 0:1] + cb_r[...]
         for k in range(1, 4):
             tap = jnp.where(dist_own[:count] >= k, xpad[pl.ds(HALO - k, count)], 0.0)
-            taps[k - 1, pl.ds(0, count)] = tap
             conv = conv + tap * cw_r[0, k:k + 1]
         sig_c = jax.nn.sigmoid(conv)
         act_b = (conv * sig_c).astype(B16)
@@ -453,15 +452,43 @@
     ex1 = Exchange(ring, g_in, lo, lambda p: dev_at(hi * g_in + p))
     ex1.start(lambda p: xin1.at[lo], lambda s: xin1.at[s])
 
-    _, vr_h, normed_h = normalise(halo[:, inner:].astype(F32))
-    ntx[...] = jnp.concatenate([normed, normed_h], axis=0).T
-    sgr[...] = jax.nn.sigmoid(pre)
-    cgr[...] = silu_grad(conv, sig_c)
-    zgr[...] = gmix * silu_grad(zgate, sig_z)
-    gsr[...] = gy * skip_r[...]
-    skr[...] = skip_r[...] * act
-    woutf[...] = dot(wout_r[...], turn_f).astype(B16)
-    gskip = jnp.sum(gy * act, axis=0, keepdims=True)
+    sub = lax.broadcasted_iota(jnp.int32, (8, LANES), 0)
+    lane_at = lax.broadcasted_iota(jnp.int32, (state, LANES), 1)
+
+    def sum_rows(v):
+        for bit in (1, 2, 4):
+            mine = lax.rem(sub // bit, 2) == 0
+            v = [
+                jnp.where(mine, a, b) + pltpu.roll(jnp.where(mine, b, a), bit, 0)
+                for a, b in zip(v[::2], v[1::2])
+            ]
+        return v[0]
+
+    halve = lambda v: v[:8] + v[8:]
+    hs[pl.ds(0, state)] = jnp.zeros((state, inner), F32)
+    pr[pl.ds(0, state)] = jnp.ones((state, inner), F32)
+
+    def prepare(g, carry):
+        h, p = list(carry[0]), list(carry[1])
+        at8 = pl.ds(pl.multiple_of(g * 8, 8), 8)
+        sa8 = sar[at8]
+        for c in range(chunks):
+            lane = slice(c * LANES, (c + 1) * LANES)
+            ys = []
+            for j in range(8):
+                at = pl.ds(pl.multiple_of((g * 8 + j) * state, state), state)
+                nxt = pl.ds(pl.multiple_of((g * 8 + j + 1) * state, state), state)
+                d, cr = dref[at, lane], bcr[at, LANES:]
+                h[c] = d * h[c] + sa8[j:j + 1, lane] * bcr[at, :LANES]
+                p[c] = p[c] * d
+                hs[nxt, lane] = h[c]
+                pr[nxt, lane] = p[c]
+                cpr[at, lane] = p[c] * cr
+                ys.append(halve(h[c] * cr))
+            yl[at8, lane] = sum_rows(ys)
+        return tuple(h), tuple(p)
+
+    lax.fori_loop(0, rows // 8, prepare, (zero, one), unroll=2)
 
     ex1.wait()
     sums = [unpair1(xin1[j]) for j in range(g_in)]
@@ -485,6 +512,21 @@
     xin2[hi] = jnp.zeros(xin2.shape[1:], B16)
     ex2 = Exchange(ring, g_out, hi, lambda p: dev_at(p * g_in + lo))
     ex2.start(lambda p: xsend2.at[jnp.where(p > hi, 0, 1)], lambda s: xin2.at[s])
+    _, vr_h, normed_h = normalise(halo[:, inner:].astype(F32))
+    for k in range(1, 4):
+        taps[k - 1] = jnp.where(dist_own >= k, xpad[pl.ds(HALO - k, rows)], 0.0)
+    ntx[...] = jnp.concatenate([normed, normed_h], axis=0).T
+    sgr[...] = jax.nn.sigmoid(pre)
+    cgr[...] = silu_grad(conv, sig_c)
+    zgr[...] = gmix * silu_grad(zgate, sig_z)
+    gsr[...] = gy * skip_r[...]
+    skr[...] = skip_r[...] * act
+    woutf[...] = dot(wout_r[...], turn_f).astype(B16)
+    gskip = jnp.sum(gy * act, axis=0, keepdims=True)
+    gpad[pl.ds(0, 8)] = jnp.zeros((8, inner), F32)
+    gpad[pl.ds(8, rows)] = gy
+    gyq[...] = gpad[pl.ds(7, rows)]
+
     ex2.wait()
     h_in = l_in = jnp.zeros((state, inner), F32)
     for k in range(g_out):
@@ -496,44 +538,21 @@
     h_in = jnp.exp2(rate2 * s_fwd) * h_in + fwd
     l_in = jnp.exp2(rate2 * s_bwd) * l_in + bwd
 
-    sub = lax.broadcasted_iota(jnp.int32, (8, LANES), 0)
-    lane_at = lax.broadcasted_iota(jnp.int32, (state, LANES), 1)
-
-    def sum_rows(v):
-        for bit in (1, 2, 4):
-            mine = lax.rem(sub // bit, 2) == 0
-            v = [
-                jnp.where(mine, a, b) + pltpu.roll(jnp.where(mine, b, a), bit, 0)
-                for a, b in zip(v[::2], v[1::2])
-            ]
-        return v[0]
-
-    halve = lambda v: v[:8] + v[8:]
-    hs[pl.ds(0, state)] = h_in
+    hin = cut(h_in)
 
     def forward(g, carry):
-        h, gc = list(carry[0]), carry[1]
         at8 = pl.ds(pl.multiple_of(g * 8, 8), 8)
-        sa8, gy8 = sar[at8], gyr[at8]
-        over = [None] * 8
         for c in range(chunks):
             lane = slice(c * LANES, (c + 1) * LANES)
             ys = []
             for j in range(8):
                 at = pl.ds(pl.multiple_of((g * 8 + j) * state, state), state)
-                nxt = pl.ds(pl.multiple_of((g * 8 + j + 1) * state, state), state)
-                h[c] = dref[at, lane] * h[c] + sa8[j:j + 1, lane] * bcr[at, :LANES]
-                hs[nxt, lane] = h[c]
-                ys.append(halve(h[c] * bcr[at, LANES:]))
-                new = h[c] * gy8[j:j + 1, lane]
-                over[j] = new if c == 0 else over[j] + new
-            yr[at8, lane] = sum_rows(ys)
-        for j in range(8):
-            gc = jnp.where(lane_at == g * 8 + j, jnp.sum(over[j], axis=1, keepdims=True), gc)
-        return tuple(h), gc
-
+                ys.append(halve(cpr[at, lane] * hin[c]))
+            yr[at8, lane] = yl[at8, lane] + sum_rows(ys)
+        return carry
+
+    lax.fori_loop(0, rows // 8, forward, 0, unroll=4)
     none = jnp.zeros((state, rows), F32)
-    _, g_c = lax.fori_loop(0, rows // 8, forward, (tuple(cut(h_in)), none), unroll=4)
     y = yr[...] + skr[...]
     mixed = (y * gate).astype(B16)
     gz = (zgr[...] * y).astype(B16)
@@ -548,11 +567,11 @@
     ring.sent.append(e_copy)
 
     def backward(i, carry):
-        m, acc, gb = list(carry[0]), list(carry[1]), carry[2]
+        m, acc, gb, gc = list(carry[0]), list(carry[1]), carry[2], carry[3]
         g = rows // 8 - 1 - i
         at8 = pl.ds(pl.multiple_of(g * 8, 8), 8)
-        sd8, gy8, sa8 = sdr[at8], gyr[at8], sar[at8]
-        over = [None] * 8
+        sd8, gy8, sa8, gq8 = sdr[at8], gyr[at8], sar[at8], gyq[at8]
+        over_b, over_c = [None] * 8, [None] * 8
         for c in range(chunks):
             lane = slice(c * LANES, (c + 1) * LANES)
             adjs, dts = [None] * 8, [None] * 8
@@ -560,24 +579,31 @@
                 at = pl.ds(pl.multiple_of((g * 8 + j) * state, state), state)
                 lam = m[c] + gy8[j:j + 1, lane] * bcr[at, LANES:]
                 m[c] = dref[at, lane] * lam
-                r = m[c] * hs[at, lane] * a1[c]
+                h = hs[at, lane] + pr[at, lane] * hin[c]
+                r = m[c] * h * a1[c]
                 acc[c] = acc[c] + r * sd8[j:j + 1, lane]
                 adjs[j] = halve(lam * bcr[at, :LANES])
                 dts[j] = halve(r)
-                new = lam * sa8[j:j + 1, lane]
-                over[j] = new if c == 0 else over[j] + new
+                new_b, new_c = lam * sa8[j:j + 1, lane], h * gq8[j:j + 1, lane]
+                over_b[j] = new_b if c == 0 else over_b[j] + new_b
+                over_c[j] = new_c if c == 0 else over_c[j] + new_c
             adjr[at8, lane] = sum_rows(adjs)
             dtar[at8, lane] = sum_rows(dts)
         for j in range(8):
-            gb = jnp.where(lane_at == g * 8 + j, jnp.sum(over[j], axis=1, keepdims=True), gb)
-        return tuple(m), tuple(acc), gb
-
-    carry = lax.fori_loop(0, rows // 32, backward, (tuple(cut(l_in)), zero, none), unroll=4)
+            t = g * 8 + j
+            gb = jnp.where(lane_at == t, jnp.sum(over_b[j], axis=1, keepdims=True), gb)
+            gc = jnp.where(lane_at == t - 1, jnp.sum(over_c[j], axis=1, keepdims=True), gc)
+        return tuple(m), tuple(acc), gb, gc
+
+    h_out = hs[pl.ds(rows * state, state)] + pr[pl.ds(rows * state, state)] * h_in
+    g_last = jnp.sum(h_out * gyr[pl.ds(rows - 1, 1)], axis=1, keepdims=True)
+    none_c = jnp.where(lane_at == rows - 1, g_last, none)
+    carry = lax.fori_loop(0, 6, backward, (tuple(cut(l_in)), zero, none, none_c), unroll=6)
     e_own = lambda at: epair[dirn, at].astype(F32) + eprecv[at].astype(F32)
     early = Sum(ring, n, seq, dirn, e_own, etotal, esend, erecv, eover, 16, E_TWO)
     e_copy.wait_recv()
     early.scatter()
-    _, galog, g_b = lax.fori_loop(rows // 32, rows // 8, backward, carry, unroll=4)
+    _, galog, g_b, g_c = lax.fori_loop(6, rows // 8, backward, carry, unroll=5)
     galog = join(galog)
     adj = adjr[...]
     gpre = (dtar[...] + adj * act) * sgr[...]
@@ -643,11 +669,16 @@
     xlate.scatter()
     if E_TWO[0]:
         early.scatter2()
+    for v, two in ((own, O_TWO), (xlate, X_TWO)):
+        if two[0]:
+            v.scatter2()
     bsend[...] = dot(dot(turn_t, mixed).astype(B16), woutf[...])
     bb = ring.take(1)
     b_copy = ring.copy(bsend, brecv, bb, bb, sibling)
     b_copy.start()
     ring.sent.append(b_copy)
+
+    early.gather()
 
     @pl.when(place < n - 1)
     def _():
@@ -667,16 +698,8 @@
     v_copy = ring.copy(vsend, vrecv, bv, bv, sibling)
     v_copy.start()
     ring.sent.append(v_copy)
-    if not E_TWO[0]:
-        early.gather()
-    for v, two in ((own, O_TWO), (xlate, X_TWO)):
-        if two[0]:
-            v.scatter2()
-    if E_TWO[0] and (X_TWO[0] or O_TWO[0]):
-        early.gather()
+
     own.gather()
-    if E_TWO[0] and not (X_TWO[0] or O_TWO[0]):
-        early.gather()
     xlate.gather()
     b_copy.wait_recv()
     out_r[...] = (tok_r[...].astype(F32) + (bsend[...] + brecv[...])).astype(B16)
@@ -786,12 +809,12 @@
         pltpu.SemaphoreType.DMA((len(ins),)),
         vm((HALO, inner + width), B16), vm((HALO, inner + width), B16),
         vm((rows * state, LANES), B16), vm((rows * state, 2 * LANES), F32),
-        vm((rows * state, inner), F32), vm(((rows + 1) * state, inner), F32),
+        *[vm((rows * state, inner), F32)] * 2, *[vm(((rows + 1) * state, inner), F32)] * 2,
         vm((rows, inner), F32), vm((rows, inner), F32), vm((rows, inner), F32),
         vm((HALO + rows, inner), F32), vm((3, rows, inner), F32), vm((3, rows + 2 * HALO, LANES), F32),
         vm((rows + HALO, inner), F32), vm((2 * HALO, inner), F32),
         vm((HALO, inner), B16), vm((HALO, inner), B16),
-        *[vm((rows, inner), F32)] * 5, vm((width, rows + HALO), B16), vm((inner, width), B16),
+        *[vm((rows, inner), F32)] * 7, vm((width, rows + HALO), B16), vm((inner, width), B16),
         vm((g_in, 2 * cells + 16, LANES), B16), vm((2, cells + 16, LANES), B16),
         vm((g_out, cells + 16, LANES), B16),
         vm((rows, inner), F32), vm((rows, inner), F32), vm((rows, inner), F32),

time: 45.3 us -> 45 us (level)
  no operation moved by 1% of the time
where the time goes in v4:
time: 45 us; the launch traced here: 44.8 us
  Pallas kernels  44.1 us (98%)
  between operations  0.66 us (1%)
    pallas_call x1, Pallas kernels, on_device(): pl.pallas_call(functools.partial(kernel, n, nsem), out_shape=mids, in_spe...  42.8 us
    pallas_call x1, Pallas kernels, on_device(): pl.pallas_call(functools.partial(finish, (w_xt.shape[1], rank, state)), o...  1.38 us

profile of v4, /device:TPU:1, one launch (start us, length us, event | category | flops | bytes accessed | tf_op | source)
XLA Modules:
  0.0 44.8 jit_solution(16536745476787982126)
XLA Ops:
  0.6 42.8 %shard_map.220 = (bf16[128,256]{1,0:T(8,128)(2,1)S(1)}, f32[128,256]{1,0:T(8,128)S(1)}, bf16[256,512]{1,0:T(8,128)(2,1)S(1)}, bf16[256,512]{1,0:T(8,128)(2,1)S(1...) custom-call(bf16[128,256]{1,0:T(8,128)(2,1)} %refs_0_.1, ...), custom_call_target="tpu_custom_call" | custom-call | tf_op jit(solution)/shard_map/pallas_call | solution.py:835
  43.4 1.4 %shard_map.221 = (bf16[128,256]{1,0:T(8,128)(2,1)}, f32[128,256]{1,0:T(8,128)}, f32[1,256]{1,0:T(1,128)}, f32[256,1024]{1,0:T(8,128)}, f32[512,256]{1,0:T(8,128)...) custom-call(bf16[128,256]{1,0:T(8,128)(2,1)S(1)} %get-tuple-element., ...), custom_call_target="tpu_custom_call" | custom-call | tf_op jit(solution)/shard_map/pallas_call | solution.py:851

commit v5 on v4

--- a/solution.py
+++ b/solution.py
@@ -762,7 +762,8 @@
     row = 0
     parts = []
     for k in (nx, ns, state, 8):
-        parts.append(jnp.concatenate([ototal[pl.ds(row, k)], ototal[pl.ds(row + k, k)]], axis=1).astype(F32))
+        both = ototal[pl.ds(row, 2 * k)].astype(F32)
+        parts.append(jnp.concatenate([both[:k], both[k:]], axis=1))
         row += 2 * k
     tail = parts[3]
     gwx[0], gwdt[0], galog[0] = parts[:3]

time: 45 us -> 45 us (level)
  no operation moved by 1% of the time
where the time goes in v5:
time: 45 us; the launch traced here: 44.8 us
  Pallas kernels  44.1 us (98%)
  between operations  0.66 us (1%)
    pallas_call x1, Pallas kernels, on_device(): pl.pallas_call(functools.partial(kernel, n, nsem), out_shape=mids, in_spe...  42.8 us
    pallas_call x1, Pallas kernels, on_device(): pl.pallas_call(functools.partial(finish, (w_xt.shape[1], rank, state)), o...  1.38 us

profile of v5, /device:TPU:1, one launch (start us, length us, event | category | flops | bytes accessed | tf_op | source)
XLA Modules:
  0.0 44.8 jit_solution(16435910150493620871)
XLA Ops:
  0.6 42.8 %shard_map.220 = (bf16[128,256]{1,0:T(8,128)(2,1)S(1)}, f32[128,256]{1,0:T(8,128)S(1)}, bf16[256,512]{1,0:T(8,128)(2,1)S(1)}, bf16[256,512]{1,0:T(8,128)(2,1)S(1...) custom-call(bf16[128,256]{1,0:T(8,128)(2,1)} %refs_0_.1, ...), custom_call_target="tpu_custom_call" | custom-call | tf_op jit(solution)/shard_map/pallas_call | solution.py:836
  43.4 1.4 %shard_map.221 = (bf16[128,256]{1,0:T(8,128)(2,1)}, f32[128,256]{1,0:T(8,128)}, f32[1,256]{1,0:T(1,128)}, f32[256,1024]{1,0:T(8,128)}, f32[512,256]{1,0:T(8,128)...) custom-call(bf16[128,256]{1,0:T(8,128)(2,1)S(1)} %get-tuple-element., ...), custom_call_target="tpu_custom_call" | custom-call | tf_op jit(solution)/shard_map/pallas_call | solution.py:852
